TPU v7x, 128 devices: a whole 4x4x4 slice. The times are simulated.
128 devices in a mesh: din: 8 (over z, core), dout: 16 (over y, x).
Axes of the slice: x: 4, y: 4, z: 4, core: 2. Of those that a mesh axis runs over, the one named last changes fastest.
Arguments:
- states: bfloat16 [1024, 16384], P(None, 'din'), may hold values from -160 to 160
- lengths: int32 [64], P('din'), may hold values from 1 to 4096, 163840 in all
- norm_gain: float32 [16384], P('din'), may hold values from 0.1 to 1.9
- query_weight: bfloat16 [16384, 16384], P('din', 'dout'), may hold values from -0.046875 to 0.046875
- keyval_weight: bfloat16 [16384, 2048], P('din', 'dout'), may hold values from -0.046875 to 0.046875
- output_weight: bfloat16 [16384, 16384], P('dout', 'din'), may hold values from -0.046875 to 0.046875
- query_scale: float32 [16384], P('dout'), may hold values from 0.5 to 2
- keyval_scale: float32 [2048], P('dout'), may hold values from 1 to 4
- output_scale: float32 [16384], P('din'), may hold values from 8 to 64
- key_cache: bfloat16 [64, 32768, 128], P('din', 'dout'), may hold values from -120 to 120
- value_cache: bfloat16 [64, 32768, 128], P('din', 'dout'), may hold values from -6 to 6
Outputs:
- attended: bfloat16 [1024, 16384], P(None, 'din')
Inputs may be any that keep to these rules, and one draw needn't show every extreme that they name: Row r's cache holds keys at positions 0 to lengths[r] - 1; its new tokens take positions lengths[r] onward.
All inputs are finite; a program needn't handle non-finite values. No bound on the sum of `lengths` on one device may be relied on, other than what follows from the above.
Results may differ from a plain program's by a relative error of at most 0.005.
The roundings to bfloat16 on the way count: a program that leaves them out, or rounds other values in their place, can miss the bound.
Values may be sent and summed in bfloat16 or wider, within the bound.
A program may use at most 128 MiB of HBM per device.

v0:
```python
import math

import jax
import jax.numpy as jnp
from jax import lax
from jax.sharding import PartitionSpec as P

D = 16384
HQ = 128
KVH = 8
HD = 128
DRAFT = 16


def swapped(value, axis, distance):
    mask = 2**distance
    pairs = [(source, source ^ mask) for source in range(lax.axis_size(axis))]
    return lax.ppermute(value, axis, pairs)


def rotary_table(head_size):
    entries = []
    for index in range(head_size // 2):
        inverse = 1.0 / 500000.0 ** (2.0 * index / head_size)
        wavelength = 2.0 * math.pi / inverse
        smooth = min(max((8192.0 / wavelength - 1.0) / 3.0, 0.0), 1.0)
        entries.append((1.0 - smooth) * inverse / 8.0 + smooth * inverse)
    return jnp.asarray(entries, dtype=jnp.float32)


def rotate(vectors, cosine, sine_part):
    halfway = vectors.shape[-1] // 2
    former = vectors[..., :halfway]
    latter = vectors[..., halfway:]
    return jnp.concatenate(
        [former * cosine - latter * sine_part, latter * cosine + former * sine_part], axis=-1
    )


def head_half(values, start, width):
    return lax.dynamic_slice_in_dim(values, start, width, 1)


def shards(
    states,
    lengths,
    norm_gain,
    query_weight,
    keyval_weight,
    output_weight,
    query_scale,
    keyval_scale,
    output_scale,
    key_cache,
    value_cache,
):
    rows_here = lengths.shape[0]
    local_rows = rows_here * DRAFT
    query_width = query_weight.shape[1]
    own_heads = query_width // HD
    group = HQ // KVH
    splits = lax.axis_size("dout") // KVH
    parity = lax.axis_index("dout") % splits
    squares = jnp.sum(jnp.square(states.astype(jnp.float32)), axis=1)
    scaled = (states.astype(jnp.float32) * norm_gain).astype(jnp.bfloat16)
    square_totals = lax.psum(squares, "din")
    own_squares = lax.dynamic_slice_in_dim(
        square_totals, lax.axis_index("din") * local_rows, local_rows, 0
    )
    summed = lax.psum_scatter(
        jnp.concatenate(
            [
                jnp.dot(scaled, query_weight, preferred_element_type=jnp.float32),
                jnp.dot(scaled, keyval_weight, preferred_element_type=jnp.float32),
            ],
            axis=1,
        ),
        "din",
        scatter_dimension=0,
        tiled=True,
    )
    inverse = lax.rsqrt(own_squares / D + 1e-05)
    queries_raw = summed[:, :query_width] * query_scale * inverse[:, None]
    pairs_raw = summed[:, query_width:] * keyval_scale * inverse[:, None]
    positions = (lengths[:, None] + jnp.arange(DRAFT, dtype=jnp.int32)[None, :]).reshape(local_rows)
    angles = positions.astype(jnp.float32)[:, None] * rotary_table(HD)[None, :]
    cosine = jnp.cos(angles)[:, None, :]
    sine_part = jnp.sin(angles)[:, None, :]
    queries = rotate(queries_raw.reshape(local_rows, own_heads, HD), cosine, sine_part).astype(
        jnp.bfloat16
    )
    turned = rotate(pairs_raw[:, None, :], cosine, sine_part)[:, 0, :]
    own_pair = jnp.where(parity == 0, turned, pairs_raw).astype(jnp.bfloat16)
    other_queries, other_pair = swapped((queries, own_pair), "dout", 0)
    group_queries = jnp.where(
        parity == 0,
        jnp.concatenate([queries, other_queries], axis=1),
        jnp.concatenate([other_queries, queries], axis=1),
    )
    new_keys = jnp.where(parity == 0, own_pair, other_pair)
    new_values = jnp.where(parity == 0, other_pair, own_pair)
    query_block = group_queries.reshape(rows_here, DRAFT, group, HD)
    key_block = new_keys.reshape(rows_here, DRAFT, HD)
    value_block = new_values.reshape(rows_here, DRAFT, HD)
    span = key_cache.shape[1]
    factor = 1.0 / math.sqrt(HD)
    cached = (
        jnp.einsum("rtgd,rpd->rgtp", query_block, key_cache, preferred_element_type=jnp.float32)
        * factor
    )
    drafted = (
        jnp.einsum("rtgd,rud->rgtu", query_block, key_block, preferred_element_type=jnp.float32)
        * factor
    )
    positions_here = parity * span + jnp.arange(span, dtype=jnp.int32)
    cache_valid = (positions_here[None, :] < lengths[:, None])[:, None, None, :]
    draft_steps = jnp.arange(DRAFT, dtype=jnp.int32)
    draft_valid = ((draft_steps[None, :] <= draft_steps[:, None]) & (parity == 0))[None, None, :, :]
    cached = jnp.where(cache_valid, cached, -1e30)
    drafted = jnp.where(draft_valid, drafted, -1e30)
    highest = jnp.maximum(
        jnp.max(cached, axis=3, keepdims=True), jnp.max(drafted, axis=3, keepdims=True)
    )
    cache_weights = jnp.where(cache_valid, jnp.exp(cached - highest), 0.0)
    draft_weights = jnp.where(draft_valid, jnp.exp(drafted - highest), 0.0)
    totals = jnp.sum(cache_weights, axis=3, keepdims=True) + jnp.sum(
        draft_weights, axis=3, keepdims=True
    )
    weighted = jnp.einsum(
        "rgtp,rpd->rgtd",
        cache_weights.astype(jnp.bfloat16),
        value_cache,
        preferred_element_type=jnp.float32,
    )
    weighted = weighted + jnp.einsum(
        "rgtu,rud->rgtd",
        draft_weights.astype(jnp.bfloat16),
        value_block,
        preferred_element_type=jnp.float32,
    )
    near_start = parity * own_heads
    far_start = (1 - parity) * own_heads
    near_high = head_half(highest, near_start, own_heads)
    near_total = head_half(totals, near_start, own_heads)
    near_weighted = head_half(weighted, near_start, own_heads)
    far_high, far_total, far_weighted = swapped(
        (
            head_half(highest, far_start, own_heads),
            head_half(totals, far_start, own_heads),
            head_half(weighted, far_start, own_heads),
        ),
        "dout",
        0,
    )
    joint = jnp.maximum(near_high, far_high)
    near_factor = jnp.exp(near_high - joint)
    far_factor = jnp.exp(far_high - joint)
    heads_out = (near_weighted * near_factor + far_weighted * far_factor) / (
        near_total * near_factor + far_total * far_factor
    )
    attention = (
        jnp.transpose(heads_out, (0, 2, 1, 3))
        .reshape(local_rows, own_heads * HD)
        .astype(jnp.bfloat16)
    )
    partial_out = jnp.dot(
        lax.all_gather(attention, "din", axis=0, tiled=True),
        output_weight,
        preferred_element_type=jnp.float32,
    )
    summed_out = lax.psum(partial_out, "dout")
    return (summed_out * output_scale).astype(jnp.bfloat16)


def solution(mesh):
    placed = (
        P(None, "din"),
        P("din"),
        P("din"),
        P("din", "dout"),
        P("din", "dout"),
        P("dout", "din"),
        P("dout"),
        P("dout"),
        P("din"),
        P("din", "dout", None),
        P("din", "dout", None),
    )
    return jax.shard_map(
        shards, mesh=mesh, in_specs=placed, out_specs=P(None, "din"), check_vma=False
    )
```

profile of v0, /device:TPU:0, one launch (start us, length us, event | category | flops | bytes accessed | tf_op | source)
XLA Modules:
  0.0 297.0 jit_solution(12081512649707719017)
XLA Ops:
  6.5 0.0 copy-start
  6.5 0.0 reduce-scatter.2.cloned.1.call-start
  6.5 1.0 copy-done
  7.6 3.9 %fusion.13 = f32[1024,128]{0,1:T(8,128)S(1)} fusion(bf16[2048,128]{1,0:T(8,128)(2,1)S(1)} %copy-done, bf16[1024,2048]{1,0:T(8,128)(2,1)} %param.12, f32[2048]{0:T(1024)} %param.14), kind=kOutput, calls=%fused_computation.19 | convolution fusion | flops 543162368 | bytes 5251072 | tf_op jit(solution)/shard_map/dot_general | solution.py:74
  11.5 0.8 copy-done.8
  12.3 4.6 %fusion.15 = f32[1024,1024]{0,1:T(8,128)S(1)} fusion(bf16[2048,1024]{1,0:T(8,128)(2,1)S(1)} %copy-done.8, bf16[1024,2048]{1,0:T(8,128)(2,1)S(1)} %copy-done.2, f32[2048]{0:T(1024)S(1)} %copy-done.10), kind=kOutput, calls=%fused_computation.20 | convolution fusion | flops 4301258752 | bytes 12591104 | tf_op jit(solution)/shard_map/dot_general | solution.py:73
  16.9 2.9 pad_maximum_fusion
  19.7 0.0 reduce-scatter.2.cloned.1.call-update
  19.8 0.0 all-gather.2.cloned.1.call-start
  19.8 0.6 copy-done.7
  20.4 0.1 add_convert_fusion.1
  20.5 0.1 convert_element_type.43
  20.5 3.1 %fusion.5 = f32[1024]{0:T(1024)S(1)} fusion(bf16[1024,2048]{1,0:T(8,128)(2,1)} %param.12), kind=kLoop, calls=%fused_computation.10 | loop fusion | flops 6290432 | bytes 4198400 | tf_op jit(solution)/shard_map/reduce_sum | solution.py:64
  23.6 16.1 %psum.14 = f32[1024]{0:T(1024)S(1)} all-reduce(f32[1024]{0:T(1024)S(1)} %fusion.5), channel_id=1, replica_groups=mesh['din'=8,'dout'=16] {'din'}, use_global_device_ids=true, to_apply=%region_2.3 | all-reduce | flops 1024 | bytes 8192 | tf_op jit(solution)/shard_map/psum | solution.py:66
  39.7 0.1 add_rsqrt_fusion
  39.8 0.2 multiply_cosine_fusion.1
  40.0 0.1 broadcast_compare_fusion
  40.1 21.5 %reduce-scatter.2.cloned.1.call-done = f32[128,1152]{0,1:T(8,128)} async-done(((f32[1024,1152]{0,1:T(8,128)}), f32[128,1152]{0,1:T(8,128)}) %reduce-scatter.2.cloned.1.call-update) | async-done | bytes 589840 | tf_op jit(solution)/shard_map/reduce_scatter | solution.py:70
  61.6 0.9 fusion.29
  62.5 0.2 fusion.34
  62.7 0.9 fusion.28
  63.6 1.5 collective-permute-start.1
  65.2 0.0 copy-done.4
  65.2 1.2 fusion.22
  66.4 0.1 subtract_convert_fusion
  66.5 0.9 collective-permute-start
  67.4 0.2 copy.45
  67.6 0.2 copy.46
  67.8 0.2 collective-permute-done.1
  68.0 0.1 copy.50
  68.1 0.1 copy.49
  68.2 4.9 %collective-permute-done = bf16[128,8,128]{0,2,1:T(8,128)(2,1)S(1)} collective-permute-done((bf16[128,8,128]{0,2,1:T(8,128)(2,1)S(1)}, bf16[128,8,128]{0,2,1:T(8,128)(2,1)S(1)}, u32[]{:S(2)}, u32[]{:S(2)}) %collective-permute-start) | collective-permute-done | bytes 262176 | tf_op jit(solution)/shard_map/ppermute | solution.py:18
  73.1 0.2 copy.47
  73.3 1.4 fusion.47
  74.8 4.7 %bitcast_reduce_fusion = (f32[8,16,16]{1,2,0:T(8,128)S(1)}, f32[8,16,16,2048]{3,2,1,0:T(8,128)S(1)}) fusion(pred[8,2048]{1,0:T(8,128)(4,1)S(1)} %broadcast_compare_fusion, bf16[8,2048,128]{2,1,0:T(8,128)(2,1)} %param.21, bf16[8,16,8,128]{3,2,1,0:T(8,128)(2,1)S(1)} %bitcast.93, bf16[8,16,8,64]{3,2,1,0:T(8,128)(2,1)S(1)} %bitcast.91, ...), kind=kOutput, calls=%fused_computation.1 | convolution fusion | flops 1089730560 | bytes 21520384 | tf_op jit(solution)/shard_map/rtgd,rpd->rgtp/dot_general | solution.py:108
  79.5 0.0 copy-start.9
  79.5 4.5 %fusion.2 = f32[8,16,16]{1,2,0:T(8,128)S(1)} fusion(f32[8,16,16,2048]{3,2,1,0:T(8,128)S(1)} %get-tuple-element.21, f32[8,16,16]{1,2,0:T(8,128)S(1)} %max.16, pred[8,2048]{1,0:T(8,128)(4,1)S(1)} %broadcast_compare_fusion), kind=kLoop, calls=%fused_computation.5 | loop fusion | flops 20969472 | bytes 16809984 | tf_op jit(solution)/shard_map/reduce_sum | solution.py:126
  84.0 4.9 %fusion.6 = f32[8,16,16,128]{3,1,2,0:T(8,128)S(1)} fusion(f32[8,16,16,2048]{3,2,1,0:T(8,128)S(1)} %get-tuple-element.21, f32[8,16,16]{1,2,0:T(8,128)S(1)} %max.16, pred[8,2048]{1,0:T(8,128)(4,1)S(1)} %broadcast_compare_fusion, bf16[8,2048,128]{2,1,0:T(8,128)(2,1)S(1)} %copy-done.9), kind=kOutput, calls=%fused_computation.12 | convolution fusion | flops 1094713344 | bytes 22044672 | tf_op jit(solution)/shard_map/rgtp,rpd->rgtd/dot_general | solution.py:129
  88.9 0.5 convolution_add_fusion
  89.4 0.7 collective-permute-start.3
  90.1 0.4 fusion.19
  90.5 0.1 constant_dynamic-slice_fusion
  90.7 0.1 copy.58
  90.7 0.1 copy.54
  90.8 1.5 collective-permute-start.2
  92.3 0.6 collective-permute-start.4
  92.9 0.1 copy.57
  92.9 0.1 copy.53
  93.0 7.4 %collective-permute-done.2 = f32[8,8,16,1]{2,1,0,3:T(8,128)S(1)} collective-permute-done((f32[8,8,16,1]{2,1,0,3:T(8,128)S(1)}, f32[8,8,16,1]{2,1,0,3:T(8,128)S(1)}, u32[]{:S(2)}, u32[]{:S(2)}) %collective-permute-start.2) | collective-permute-done | bytes 4128 | tf_op jit(solution)/shard_map/ppermute | solution.py:18
  100.4 0.4 collective-permute-done.4
  100.8 0.1 copy.55
  100.9 0.1 copy.59
  100.9 0.1 copy.56
  101.0 0.0 collective-permute-done.3
  101.0 0.5 divide_convert_fusion
  101.5 0.8 copy.69
  102.3 0.0 all-gather.2.cloned.1.call-update
  102.3 0.3 all-reduce.2.cloned.1.call-start
  102.6 28.9 %all-gather.2.cloned.1.call-done = bf16[1024,1024]{1,0:T(8,128)(2,1)} async-done(((bf16[128,1024]{1,0:T(8,128)(2,1)}), bf16[1024,1024]{1,0:T(8,128)(2,1)}) %all-gather.2.cloned.1.call-update) | async-done | bytes 2097168 | tf_op jit(solution)/shard_map/all_gather | solution.py:167
  131.5 10.5 %fusion.48 = f32[1024,2048]{1,0:T(8,128)} fusion(bf16[1024,1024]{1,0:T(8,128)(2,1)} %all-gather.2.cloned.1.call-done, bf16[1024,2048]{1,0:T(8,128)(2,1)} %param.17), kind=kOutput, calls=%fused_computation.82 | convolution fusion | flops 4294967296 | bytes 14680064 | tf_op jit(solution)/shard_map/dot_general | solution.py:166
  142.0 0.0 all-reduce.2.cloned.1.call-update
  142.1 0.0 copy-start.1
  142.1 141.8 %all-reduce.2.cloned.1.call-done = f32[1024,2048]{1,0:T(8,128)} async-done(((f32[1024,2048]{1,0:T(8,128)}), f32[1024,2048]{1,0:T(8,128)}) %all-reduce.2.cloned.1.call-update) | async-done | bytes 8388624 | tf_op jit(solution)/shard_map/psum | solution.py:171
  283.9 6.6 %multiply_convert_fusion = bf16[1024,2048]{1,0:T(8,128)(2,1)} fusion(f32[1024,2048]{1,0:T(8,128)} %all-reduce.2.cloned.1.call-done, f32[2048]{0:T(1024)S(1)} %copy-done.3), kind=kLoop, calls=%fused_computation.11 | loop fusion | flops 4194304 | bytes 12591104 | tf_op jit(solution)/shard_map/convert_element_type | solution.py:172
  (23 shorter events, 0.2 us)
Async XLA Ops:
  6.5 1.0 copy-start
  6.5 4.9 %copy-start.10 = (f32[2048]{0:T(1024)S(1)}, f32[2048]{0:T(1024)}, u32[]{:S(2)}) copy-start(f32[2048]{0:T(1024)} %param.14) | copy-start | bytes 24580
  6.5 55.0 %reduce-scatter.2.cloned.1.call-start = ((), (), s32[]{:S(2)}) async-start(), calls=%async_computation.1 | async-start | bytes 5308416 | tf_op jit(solution)/shard_map/reduce_scatter | solution.py:70
  7.6 3.9 %copy-start.2 = (bf16[1024,2048]{1,0:T(8,128)(2,1)S(1)}, bf16[1024,2048]{1,0:T(8,128)(2,1)}, u32[]{:S(2)}) copy-start(bf16[1024,2048]{1,0:T(8,128)(2,1)} %param.12) | copy-start | bytes 12582916
  7.6 4.7 %copy-start.8 = (bf16[2048,1024]{1,0:T(8,128)(2,1)S(1)}, bf16[2048,1024]{1,0:T(8,128)(2,1)}, u32[]{:S(2)}) copy-start(bf16[2048,1024]{1,0:T(8,128)(2,1)} %param.15) | copy-start | bytes 12582916
  19.7 0.7 copy-start.7
  19.7 20.1 %copy-start.6 = (f32[64]{0:T(128)S(1)}, f32[64]{0:T(128)}, u32[]{:S(2)}) copy-start(f32[64]{0:T(128)} %constant.50.clone) | copy-start | bytes 772
  19.7 41.8 %copy-start.5 = (f32[128]{0:T(128)S(1)}, f32[128]{0:T(128)}, u32[]{:S(2)}) copy-start(f32[128]{0:T(128)} %param.19) | copy-start | bytes 1540
  19.7 45.4 %copy-start.4 = (f32[1024]{0:T(1024)S(1)}, f32[1024]{0:T(1024)}, u32[]{:S(2)}) copy-start(f32[1024]{0:T(1024)} %param.18) | copy-start | bytes 12292
  19.8 111.7 %all-gather.2.cloned.1.call-start = ((), (), s32[]{:S(2)}) async-start(), calls=%async_computation.2 | async-start | bytes 2359296 | tf_op jit(solution)/shard_map/all_gather | solution.py:167
  63.6 4.4 %collective-permute-start.1 = (bf16[128,128]{0,1:T(8,128)(2,1)S(1)}, bf16[128,128]{0,1:T(8,128)(2,1)S(1)}, u32[]{:S(2)}, u32[]{:S(2)}) collective-permute-start(bf16[128,128]{0,1:T(8,128)(2,1)S(1)} %fusion.28), channel_id=1, source_target_pairs={{0,1},{1,0},{2,3},{3,2},{4,5},{5,4},{6,7},{7,6},{8,9},{9,8},{10,11... | collective-permute-start | bytes 98312 | tf_op jit(solution)/shard_map/ppermute | solution.py:18
  66.5 6.6 %collective-permute-start = (bf16[128,8,128]{0,2,1:T(8,128)(2,1)S(1)}, bf16[128,8,128]{0,2,1:T(8,128)(2,1)S(1)}, u32[]{:S(2)}, u32[]{:S(2)}) collective-permute-start(bf16[128,8,128]{0,2,1:T(8,128)(2,1)S(1)} %pad_maximum_fusion.1), channel_id=1, source_target_pairs={{0,1},{1,0},{2,3},{3,2},{4,5},{5,4},{6,7},{7,6},{8,9},{9,8},{10,11... | collective-permute-start | bytes 786440 | tf_op jit(solution)/shard_map/ppermute | solution.py:18
  79.5 4.5 %copy-start.9 = (bf16[8,2048,128]{2,1,0:T(8,128)(2,1)S(1)}, bf16[8,2048,128]{2,1,0:T(8,128)(2,1)}, u32[]{:S(2)}) copy-start(bf16[8,2048,128]{2,1,0:T(8,128)(2,1)} %param.22) | copy-start | bytes 12582916
  89.4 11.6 %collective-permute-start.3 = (f32[8,8,16,128]{3,1,2,0:T(8,128)S(1)}, f32[8,8,16,128]{3,1,2,0:T(8,128)S(1)}, u32[]{:S(2)}, u32[]{:S(2)}) collective-permute-start(f32[8,8,16,128]{3,1,2,0:T(8,128)S(1)} %constant_dynamic-slice_fusion.2), channel_id=1, source_target_pairs={{0,1},{1,0},{2,3},{3,2},{4,5},{5,4},{6,7},{7,6},{8,9},{9,8},{10,11... | collective-permute-start | bytes 1572872 | tf_op jit(solution)/shard_map/ppermute | solution.py:18
  90.8 9.6 %collective-permute-start.2 = (f32[8,8,16,1]{2,1,0,3:T(8,128)S(1)}, f32[8,8,16,1]{2,1,0,3:T(8,128)S(1)}, u32[]{:S(2)}, u32[]{:S(2)}) collective-permute-start(f32[8,8,16,1]{2,1,0,3:T(8,128)S(1)} %bitcast.98), channel_id=1, source_target_pairs={{0,1},{1,0},{2,3},{3,2},{4,5},{5,4},{6,7},{7,6},{8,9},{9,8},{10,11... | collective-permute-start | bytes 12296 | tf_op jit(solution)/shard_map/ppermute | solution.py:18
  92.3 8.5 %collective-permute-start.4 = (f32[8,8,16,1]{2,1,0,3:T(8,128)S(1)}, f32[8,8,16,1]{2,1,0,3:T(8,128)S(1)}, u32[]{:S(2)}, u32[]{:S(2)}) collective-permute-start(f32[8,8,16,1]{2,1,0,3:T(8,128)S(1)} %bitcast.97), channel_id=1, source_target_pairs={{0,1},{1,0},{2,3},{3,2},{4,5},{5,4},{6,7},{7,6},{8,9},{9,8},{10,11... | collective-permute-start | bytes 12296 | tf_op jit(solution)/shard_map/ppermute | solution.py:18
  102.3 181.6 %all-reduce.2.cloned.1.call-start = ((), (), s32[]{:S(2)}) async-start(), calls=%async_computation.3 | async-start | bytes 16777216 | tf_op jit(solution)/shard_map/psum | solution.py:171
  142.0 141.8 %copy-start.3 = (f32[2048]{0:T(1024)S(1)}, f32[2048]{0:T(1024)}, u32[]{:S(2)}) copy-start(f32[2048]{0:T(1024)} %param.20) | copy-start | bytes 24580
  142.1 148.4 %copy-start.1 = (bf16[2048,128]{1,0:T(8,128)(2,1)S(1)}, bf16[2048,128]{1,0:T(8,128)(2,1)}, u32[]{:S(2)}) copy-start(bf16[2048,128]{1,0:T(8,128)(2,1)} %param.16) | copy-start | bytes 1572868
Sparse Core Ops, SparseCore 0:
  19.9 41.6 reduce-scatter.1
  102.4 29.0 all-gather.1
  142.2 141.6 all-reduce.1
where the time goes:
time: 298 us; the launch traced here: 297 us
  waiting for transfers between devices  205 us (69%)
  matrix products  30.5 us (10%)
  other arithmetic  21.7 us (7%)
  blocking collectives  16.1 us (5%)
  between operations  13.3 us (4%)
  starting transfers between devices  5.4 us (2%)
  local copies, waits for them, and re-layouts  4.81 us (2%)
    psum x1, waiting for transfers between devices, shards(): summed_out = lax.psum(partial_out, 'dout')  142 us
    all_gather x1, waiting for transfers between devices, shards(): lax.all_gather(attention, 'din', axis=0, tiled=True)  28.9 us
    reduce_scatter x1, waiting for transfers between devices, shards(): lax.psum_scatter(jnp.concatenate([jnp.dot(scaled, query_weight, preferred...  21.5 us
    psum x1, blocking collectives, shards(): square_totals = lax.psum(squares, 'din')  16.1 us
    ppermute x5, waiting for transfers between devices, swapped(): return lax.ppermute(value, axis, pairs)  12.9 us
    dot_general x1, matrix products, shards(): jnp.dot(lax.all_gather(attention, 'din', axis=0, tiled=True), output_weig...  10.5 us
    convert_element_type x1, other arithmetic, shards(): return (summed_out * output_scale).astype(jnp.bfloat16)  6.55 us
  transfers between devices with their start and end apart: 8, of which 7 were waited for; matrix products, arithmetic and copies ran while one was open for 2% of the time, Pallas kernels for 0%

commit v1 on v0

v1 whole, which is shorter than its diff:
```python
import functools
import math

import jax
import jax.numpy as jnp
from jax import lax
from jax.experimental import pallas as pl
from jax.experimental.pallas import tpu as pltpu
from jax.sharding import PartitionSpec as P

D = 16384
HQ = 128
KVH = 8
HD = 128
DRAFT = 16
ROWS_HERE = 8
OWN = 8
QW = OWN * HD
WIDE = QW + 2 * HD
SPAN = 2048
FEATS = 2048
OUTS = 2048

CHUNK_ROWS = 2
NC = ROWS_HERE // CHUNK_ROWS
T = CHUNK_ROWS * DRAFT
NB = 8
M = NB * T
LOG_SCALE = math.log2(math.e) / math.sqrt(HD)
LOWEST = -1e30

CORE = 0
ZRS = 1
SWAP = 7
FAR = 9
ZAG = FAR + CHUNK_ROWS
CAG = ZAG + 4
RS1 = CAG + 4
RS2 = RS1 + 12
AG2 = RS2 + 12
AG1 = AG2 + 8
NSEM = AG1 + 8


def rotary_table(head_size):
    entries = []
    for index in range(head_size // 2):
        inverse = 1.0 / 500000.0 ** (2.0 * index / head_size)
        wavelength = 2.0 * math.pi / inverse
        smooth = min(max((8192.0 / wavelength - 1.0) / 3.0, 0.0), 1.0)
        entries.append((1.0 - smooth) * inverse / 8.0 + smooth * inverse)
    return jnp.asarray(entries, dtype=jnp.float32)


def mod4(v):
    return lax.rem(v, 4)


def f32(v):
    return v.astype(jnp.float32)


def kernel(
    lengths, gain, qscale, kvscale, oscale, cosines, sines,
    states, wq, wkv, wo, keys, values,
    out,
    xs, wq_v, wkv_v, wo_v, k_v, v_v, scaled,
    ybuf, crecv, zrecv, qbuf, kvbuf, kpad, vpad, obuf, orecv, gat,
    pbuf, r1, gf, gb, r2, outb,
    load_sem, send_sem, recv_sem, store_sem,
):
    din = lax.axis_index("din")
    dout = lax.axis_index("dout")
    core = lax.rem(din, 2)
    z = lax.div(din, 2)
    x = lax.rem(dout, 4)
    y = lax.div(dout, 4)
    parity = lax.rem(x, 2)
    core_peer = (din + 1 - 2 * core, dout)
    pair_peer = (din, dout + 1 - 2 * parity)
    z_plus = (lax.rem(din + 2, 8), dout)
    z_minus = (lax.rem(din + 6, 8), dout)
    x_plus = (din, 4 * y + mod4(x + 1))
    x_minus = (din, 4 * y + mod4(x + 3))
    y_plus = (din, lax.rem(dout + 4, 16))
    y_minus = (din, lax.rem(dout + 12, 16))
    neighbours = (core_peer, z_plus, z_minus, x_plus, x_minus, y_plus, y_minus)

    def load(src, dst, index):
        return pltpu.make_async_copy(src, dst, load_sem.at[index])

    def states_load(c):
        return load(states.at[:, pl.ds(c * T, T), :], xs.at[c], c)

    wq_load = load(wq, wq_v, NC)
    wkv_load = load(wkv, wkv_v, NC + 1)
    wo_load = load(wo, wo_v, NC + 2)
    k_load = load(keys, k_v, NC + 3)
    v_load = load(values, v_v, NC + 4)
    states_load(0).start()
    wq_load.start()
    wkv_load.start()
    for c in range(1, NC):
        states_load(c).start()
    k_load.start()
    v_load.start()
    wo_load.start()

    barrier = pltpu.get_barrier_semaphore()
    for peer in neighbours:
        pl.semaphore_signal(barrier, inc=1, device_id=peer, device_id_type=pl.DeviceIdType.MESH)
    pl.semaphore_wait(barrier, len(neighbours))

    started = []

    def remote(src, dst, row, c, peer):
        return pltpu.make_async_remote_copy(
            src_ref=src,
            dst_ref=dst,
            send_sem=send_sem.at[row, c],
            recv_sem=recv_sem.at[row, c],
            device_id=peer,
            device_id_type=pl.DeviceIdType.MESH,
        )

    def send(src, dst, row, c, peer):
        copy = remote(src, dst, row, c, peer)
        copy.start()
        started.append(copy)

    def arrived(dst, row, c):
        remote(dst, dst, row, c, core_peer).wait_recv()

    def scatter_start(base, c, shard, land, index, plus, minus):
        far = mod4(index + 2)
        send(shard(far, 1), land(0), base, c, plus)
        send(shard(far, 0), land(1), base + 1, c, minus)
        send(shard(mod4(index + 1), 0), land(2), base + 2, c, plus)
        send(shard(mod4(index + 3), 1), land(3), base + 3, c, minus)

    def scatter_mid(base, c, shard, land, index, plus, minus, own=None):
        own = own or shard
        for slot, step, half, peer in ((0, 1, 1, plus), (1, 3, 0, minus)):
            target = mod4(index + step)
            arrived(land(slot), base + slot, c)
            piece = shard(target, half)
            piece[...] = (f32(own(target, half)[...]) + f32(land(slot)[...])).astype(piece.dtype)
            send(piece, land(4 + slot), base + 4 + slot, c, peer)

    def scatter_end(base, c, shard, land, index):
        halves = []
        for half, direct, chained in ((0, 2, 5), (1, 3, 4)):
            arrived(land(direct), base + direct, c)
            arrived(land(chained), base + chained, c)
            halves.append(
                f32(shard(index, half)[...]) + f32(land(direct)[...]) + f32(land(chained)[...])
            )
        return halves

    def gather_start(base, c, part, index, plus, minus):
        own = part(index, None)
        send(own, own, base, c, plus)
        send(own, own, base + 1, c, minus)

    def gather_mid(base, c, part, index, plus, minus):
        for slot, step, half, peer in ((0, 3, 0, plus), (1, 1, 1, minus)):
            source = mod4(index + step)
            arrived(part(source, None), base + slot, c)
            piece = part(source, half)
            send(piece, piece, base + 2 + slot, c, peer)

    def gather_end(base, c, part, index):
        far = mod4(index + 2)
        arrived(part(far, 0), base + 2, c)
        arrived(part(far, 1), base + 3, c)

    def z_shard(c):
        return lambda t, h: ybuf.at[c, core, t, pl.ds(h * (T // 2), T // 2), :]

    def z_land(c):
        return lambda slot: zrecv.at[c, slot]

    def project(c):
        states_load(c).wait()
        wide = f32(xs[c]).reshape(M, FEATS)
        squares = jnp.sum(wide * wide, axis=1, keepdims=True)
        scaled[...] = (wide * gain[...]).astype(jnp.bfloat16)
        if c == 0:
            wq_load.wait()
            wkv_load.wait()

        def put(block, start):
            for b in range(NB):
                ybuf[c, b % 2, b // 2, :, start] = block[b * T : (b + 1) * T]

        put(jnp.broadcast_to(squares, (M, HD)), pl.ds(QW + HD, HD))
        put(
            jnp.dot(scaled[...], wkv_v[...], preferred_element_type=jnp.float32), pl.ds(QW, HD)
        )

        @pl.loop(0, QW // 256)
        def _(j):
            start = pl.ds(pl.multiple_of(j * 256, 256), 256)
            put(
                jnp.dot(scaled[...], wq_v[:, start], preferred_element_type=jnp.float32), start
            )

        send(ybuf.at[c, 1 - core], crecv.at[c], CORE, c, core_peer)

    def pair_cores(c):
        arrived(crecv.at[c], CORE, c)
        ybuf[c, core] = ybuf[c, core] + crecv[c]
        scatter_start(ZRS, c, z_shard(c), z_land(c), z, z_plus, z_minus)

    def project_mid(c):
        scatter_mid(ZRS, c, z_shard(c), z_land(c), z, z_plus, z_minus)

    def project_end(c):
        total = jnp.concatenate(scatter_end(ZRS, c, z_shard(c), z_land(c), z), axis=0)
        inverse = lax.rsqrt(total[:, QW + HD :] / D + 1e-05)
        cosine = cosines[c]
        sine = sines[c]
        half = HD // 2
        for h in range(OWN):
            cols = slice(h * HD, (h + 1) * HD)
            raw = total[:, cols] * qscale[:, cols] * inverse
            turned = jnp.concatenate([raw[:, half:], raw[:, :half]], axis=1)
            query = (raw * cosine + turned * sine).astype(jnp.bfloat16)
            for r in range(CHUNK_ROWS):
                qbuf[c, parity, r, pl.ds(h * DRAFT, DRAFT), :] = query[
                    r * DRAFT : (r + 1) * DRAFT
                ]
        raw = total[:, QW : QW + HD] * kvscale[...] * inverse
        turned = jnp.concatenate([raw[:, half:], raw[:, :half]], axis=1)
        rotated = raw * cosine + turned * sine
        kvbuf[c, parity] = jnp.where(parity == 0, rotated, raw).astype(jnp.bfloat16)
        send(qbuf.at[c, parity], qbuf.at[c, parity], SWAP, c, pair_peer)
        send(kvbuf.at[c, parity], kvbuf.at[c, parity], SWAP + 1, c, pair_peer)

    def attend(c):
        if c == 0:
            kpad[...] = jnp.zeros_like(kpad)
            vpad[...] = jnp.zeros_like(vpad)
            k_load.wait()
            v_load.wait()
        arrived(qbuf.at[c, 1 - parity], SWAP, c)
        arrived(kvbuf.at[c, 1 - parity], SWAP + 1, c)
        place = lax.broadcasted_iota(jnp.int32, (1, SPAN), 1) + parity * SPAN
        token = lax.rem(lax.broadcasted_iota(jnp.int32, (2 * OWN * DRAFT, HD), 0), DRAFT)
        other = lax.broadcasted_iota(jnp.int32, (2 * OWN * DRAFT, HD), 1)
        drafted = (other <= token) & (parity == 0)
        lane = lax.broadcasted_iota(jnp.int32, (QW // OWN, HD), 1)
        for r in range(CHUNK_ROWS):
            row = c * CHUNK_ROWS + r
            kpad[0:DRAFT] = kvbuf[c, 0, r * DRAFT : (r + 1) * DRAFT]
            vpad[0:DRAFT] = kvbuf[c, 1, r * DRAFT : (r + 1) * DRAFT]
            query = jnp.concatenate([qbuf[c, 0, r], qbuf[c, 1, r]], axis=0)
            across = (((1,), (1,)), ((), ()))
            bias = jnp.where(place < lengths[row], 0.0, LOWEST)
            scores = (
                lax.dot_general(query, k_v[row], across, preferred_element_type=jnp.float32)
                * LOG_SCALE
                + bias
            )
            fresh = lax.dot_general(query, kpad[...], across, preferred_element_type=jnp.float32)
            fresh = jnp.where(drafted, fresh * LOG_SCALE, LOWEST)
            top = jnp.maximum(
                jnp.max(scores, axis=1, keepdims=True), jnp.max(fresh, axis=1, keepdims=True)
            )
            weights = jnp.exp2(scores - top)
            fresh_weights = jnp.exp2(fresh - top)
            totals = jnp.sum(weights, axis=1, keepdims=True) + jnp.sum(
                fresh_weights, axis=1, keepdims=True
            )
            weighted = jnp.dot(
                weights.astype(jnp.bfloat16), v_v[row], preferred_element_type=jnp.float32
            ) + jnp.dot(
                fresh_weights.astype(jnp.bfloat16), vpad[...], preferred_element_type=jnp.float32
            )
            for p in range(2):
                mine = slice(p * QW // OWN, (p + 1) * QW // OWN)
                both = jnp.where(lane < HD // 2, top[mine], totals[mine]).T
                obuf[c, p, r, 0:HD] = weighted[mine]
                obuf[c, p, r, HD : HD + 8] = both[0:8]
                obuf[c, p, r, HD + 8 : HD + 16] = both[HD // 2 : HD // 2 + 8]
            send(obuf.at[c, 1 - parity, r], orecv.at[c, r], FAR + r, c, pair_peer)

    def att_part(c):
        def part(t, half):
            if half is None:
                return gat.at[c, 2 * t + core]
            return gat.at[c, 2 * t + core, :, pl.ds(half * (QW // 2), QW // 2)]

        return part

    def to_core(c, slot, t):
        block = gat.at[c, 2 * t + core]
        send(block, block, CAG + slot, c, core_peer)

    def combine(c):
        for r in range(CHUNK_ROWS):
            arrived(orecv.at[c, r], FAR + r, c)
            near_top = obuf[c, parity, r, HD : HD + 8]
            near_total = obuf[c, parity, r, HD + 8 : HD + 16]
            far_top = orecv[c, r, HD : HD + 8]
            far_total = orecv[c, r, HD + 8 : HD + 16]
            joint = jnp.maximum(near_top, far_top)
            near_factor = jnp.exp2(near_top - joint)
            far_factor = jnp.exp2(far_top - joint)
            share = 1.0 / (near_total * near_factor + far_total * far_factor)

            def spread(factor):
                return jnp.broadcast_to((factor * share)[0:1], (HD, HD)).T

            heads = (
                obuf[c, parity, r, 0:HD] * spread(near_factor)
                + orecv[c, r, 0:HD] * spread(far_factor)
            ).astype(jnp.bfloat16)
            for h in range(OWN):
                gat[c, din, r * DRAFT : (r + 1) * DRAFT, h * HD : (h + 1) * HD] = heads[
                    h * DRAFT : (h + 1) * DRAFT
                ]
        gather_start(ZAG, c, att_part(c), z, z_plus, z_minus)
        to_core(c, 0, z)

    def gather_heads(c):
        gather_mid(ZAG, c, att_part(c), z, z_plus, z_minus)
        to_core(c, 1, mod4(z + 3))
        to_core(c, 2, mod4(z + 1))

    def gather_far_heads(c):
        gather_end(ZAG, c, att_part(c), z)
        to_core(c, 3, mod4(z + 2))

    first = ((x, x_plus, x_minus), (y, y_plus, y_minus))
    second = ((y, y_plus, y_minus), (x, x_plus, x_minus))

    def columns(side, t):
        return pl.ds(pl.multiple_of(side * (OUTS // 2) + t * 256, 256), 256)

    def shard1(c, side):
        return lambda t, h: pbuf.at[c, pl.ds(h * 4, 4), :, columns(side, t)]

    def land1(c, side):
        return lambda slot: r1.at[c, side, slot]

    def shard2(c, side, buffer):
        return lambda t, h: buffer.at[c, side, 2 * t + h]

    def land2(c, side):
        return lambda slot: r2.at[c, side, slot]

    def part2(c, side):
        def part(t, half):
            place = columns(side, first[side][0])
            if half is None:
                return outb.at[c, pl.ds(2 * t, 2), :, place]
            return outb.at[c, pl.ds(2 * t + half, 1), :, place]

        return part

    def part1(c, side):
        def part(t, half):
            if half is None:
                return outb.at[c, :, :, columns(side, t)]
            return outb.at[c, pl.ds(half * 4, 4), :, columns(side, t)]

        return part

    def output(c):
        if c == 0:
            wo_load.wait()
        for slot, step in enumerate((0, 3, 1, 2)):
            t = mod4(z + step)
            arrived(gat.at[c, 2 * t + 1 - core], CAG + slot, c)

        @pl.loop(0, OUTS // 256)
        def _(j):
            cols = pl.ds(pl.multiple_of(j * 256, 256), 256)
            block = jnp.dot(
                gat[c].reshape(M, QW), wo_v[:, cols], preferred_element_type=jnp.float32
            )
            pbuf[c, :, :, cols] = block.astype(jnp.bfloat16).reshape(NB, T, 256)

        for side in range(2):
            scatter_start(RS1 + 6 * side, c, shard1(c, side), land1(c, side), *first[side])

    def sum_mid(c):
        for side in range(2):
            scatter_mid(RS1 + 6 * side, c, shard1(c, side), land1(c, side), *first[side])

    def sum_end(c):
        for side in range(2):
            halves = scatter_end(
                RS1 + 6 * side, c, shard1(c, side), land1(c, side), first[side][0]
            )
            for h in range(2):
                gf[c, side, h * 4 : (h + 1) * 4] = halves[h]
                gb[c, side, h * 4 : (h + 1) * 4] = halves[h].astype(jnp.bfloat16)
            scatter_start(
                RS2 + 6 * side, c, shard2(c, side, gb), land2(c, side), *second[side]
            )

    def cross_mid(c):
        for side in range(2):
            scatter_mid(
                RS2 + 6 * side,
                c,
                shard2(c, side, gb),
                land2(c, side),
                *second[side],
                own=shard2(c, side, gf),
            )

    def cross_end(c):
        for side in range(2):
            index = second[side][0]
            halves = scatter_end(
                RS2 + 6 * side, c, shard2(c, side, gf), land2(c, side), index
            )
            cols = columns(side, first[side][0])
            for h in range(2):
                outb[c, 2 * index + h, :, cols] = (halves[h] * oscale[:, cols]).astype(
                    jnp.bfloat16
                )
            gather_start(AG2 + 4 * side, c, part2(c, side), *second[side])

    def spread_mid(c):
        for side in range(2):
            gather_mid(AG2 + 4 * side, c, part2(c, side), *second[side])

    def spread_end(c):
        for side in range(2):
            gather_end(AG2 + 4 * side, c, part2(c, side), second[side][0])
            gather_start(AG1 + 4 * side, c, part1(c, side), *first[side])

    def last_mid(c):
        for side in range(2):
            gather_mid(AG1 + 4 * side, c, part1(c, side), *first[side])

    def out_store(c):
        return pltpu.make_async_copy(
            outb.at[c], out.at[:, pl.ds(c * T, T), :], store_sem.at[c]
        )

    def last_end(c):
        for side in range(2):
            gather_end(AG1 + 4 * side, c, part1(c, side), first[side][0])
        out_store(c).start()

    stages = (
        (project, 0.0, 1.6),
        (pair_cores, 1.8, 2.0),
        (project_mid, 6.0, 5.0),
        (project_end, 8.5, 5.0),
        (attend, 11.0, 5.5),
        (combine, 14.0, 5.5),
        (gather_heads, 16.5, 5.5),
        (gather_far_heads, 18.5, 5.5),
        (output, 20.0, 9.0),
        (sum_mid, 23.5, 9.6),
        (sum_end, 26.0, 9.6),
        (cross_mid, 28.0, 9.6),
        (cross_end, 30.0, 9.6),
        (spread_mid, 32.0, 9.6),
        (spread_end, 34.0, 9.6),
        (last_mid, 37.0, 9.6),
        (last_end, 40.0, 9.6),
    )
    order = sorted(
        (begin + c * gap, i, c) for i, (_, begin, gap) in enumerate(stages) for c in range(NC)
    )
    for _, i, c in order:
        stages[i][0](c)

    for c in range(NC):
        out_store(c).wait()
    for copy in started:
        copy.wait_send()


def shards(
    states,
    lengths,
    norm_gain,
    query_weight,
    keyval_weight,
    output_weight,
    query_scale,
    keyval_scale,
    output_scale,
    key_cache,
    value_cache,
):
    positions = (lengths[:, None] + jnp.arange(DRAFT, dtype=jnp.int32)[None, :]).reshape(NC, T, 1)
    angles = positions.astype(jnp.float32) * rotary_table(HD)
    cosine = jnp.cos(angles)
    sine = jnp.sin(angles)
    cosines = jnp.concatenate([cosine, cosine], axis=2)
    sines = jnp.concatenate([-sine, sine], axis=2)
    bf16 = jnp.bfloat16
    vmem = pl.BlockSpec(memory_space=pltpu.VMEM)
    smem = pl.BlockSpec(memory_space=pltpu.SMEM)
    hbm = pl.BlockSpec(memory_space=pl.ANY)
    result = pl.pallas_call(
        kernel,
        out_shape=jax.ShapeDtypeStruct((NB, ROWS_HERE * DRAFT, OUTS), bf16),
        in_specs=[smem] + [vmem] * 6 + [hbm] * 6,
        out_specs=hbm,
        scratch_shapes=[
            pltpu.VMEM((NC, NB, T, FEATS), bf16),
            pltpu.VMEM((FEATS, QW), bf16),
            pltpu.VMEM((FEATS, HD), bf16),
            pltpu.VMEM((QW, OUTS), bf16),
            pltpu.VMEM((ROWS_HERE, SPAN, HD), bf16),
            pltpu.VMEM((ROWS_HERE, SPAN, HD), bf16),
            pltpu.VMEM((M, FEATS), bf16),
            pltpu.VMEM((NC, 2, 4, T, WIDE), jnp.float32),
            pltpu.VMEM((NC, 4, T, WIDE), jnp.float32),
            pltpu.VMEM((NC, 6, T // 2, WIDE), jnp.float32),
            pltpu.VMEM((NC, 2, CHUNK_ROWS, OWN * DRAFT, HD), bf16),
            pltpu.VMEM((NC, 2, T, HD), bf16),
            pltpu.VMEM((HD, HD), bf16),
            pltpu.VMEM((HD, HD), bf16),
            pltpu.VMEM((NC, 2, CHUNK_ROWS, HD + 16, HD), jnp.float32),
            pltpu.VMEM((NC, CHUNK_ROWS, HD + 16, HD), jnp.float32),
            pltpu.VMEM((NC, NB, T, QW), bf16),
            pltpu.VMEM((NC, NB, T, OUTS), bf16),
            pltpu.VMEM((NC, 2, 6, 4, T, 256), bf16),
            pltpu.VMEM((NC, 2, NB, T, 256), jnp.float32),
            pltpu.VMEM((NC, 2, NB, T, 256), bf16),
            pltpu.VMEM((NC, 2, 6, T, 256), bf16),
            pltpu.VMEM((NC, NB, T, OUTS), bf16),
            pltpu.SemaphoreType.DMA((NC + 5,)),
            pltpu.SemaphoreType.DMA((NSEM, NC)),
            pltpu.SemaphoreType.DMA((NSEM, NC)),
            pltpu.SemaphoreType.DMA((NC,)),
        ],
        compiler_params=pltpu.CompilerParams(
            collective_id=0, has_side_effects=True, vmem_limit_bytes=63 * 2**20
        ),
        cost_estimate=pl.CostEstimate(
            flops=12 * 10**9, bytes_accessed=25 * 2**20, transcendentals=2**22
        ),
    )(
        lengths,
        norm_gain[None, :],
        query_scale[None, :],
        keyval_scale[None, :],
        output_scale[None, :],
        cosines,
        sines,
        states.reshape(NB, ROWS_HERE * DRAFT, FEATS),
        query_weight,
        keyval_weight,
        output_weight,
        key_cache,
        value_cache,
    )
    return result.reshape(NB * ROWS_HERE * DRAFT, OUTS)


def solution(mesh):
    placed = (
        P(None, "din"),
        P("din"),
        P("din"),
        P("din", "dout"),
        P("din", "dout"),
        P("dout", "din"),
        P("dout"),
        P("dout"),
        P("din"),
        P("din", "dout", None),
        P("din", "dout", None),
    )
    return jax.shard_map(
        shards, mesh=mesh, in_specs=placed, out_specs=P(None, "din"), check_vma=False
    )
```

time: 298 us -> 148 us (0.50)
  waiting for transfers between devices: 205 us -> 0 us
  Pallas kernels: 0 us -> 141 us
  matrix products: 30.5 us -> 0 us
  other arithmetic: 21.7 us -> 1.73 us
  blocking collectives: 16.1 us -> 0 us
  between operations: 13.3 us -> 0.02 us
  starting transfers between devices: 5.4 us -> 0 us
    psum x1 -> x0, waiting for transfers between devices: 142 us -> none  [shards(): summed_out = lax.psum(partial_out, 'dout')]
    pallas_call x0 -> x1, Pallas kernels: none -> 141 us  [shards(): pl.pallas_call(kernel, out_shape=jax.ShapeDtypeStruct((NB, ROWS_HERE * DR...]
    dot_general x7 -> x0, matrix products: 30.5 us -> none  [the longest x1 10.5 us: shards(): jnp.dot(lax.all_gather(attention, 'din', axis=0, tiled=True), output_weig...]
    all_gather x1 -> x0, waiting for transfers between devices: 28.9 us -> none  [shards(): lax.all_gather(attention, 'din', axis=0, tiled=True)]
    reduce_scatter x1 -> x0, waiting for transfers between devices: 21.5 us -> none  [shards(): lax.psum_scatter(jnp.concatenate([jnp.dot(scaled, query_weight, preferred...]
    psum x1 -> x0, blocking collectives: 16.1 us -> none  [shards(): square_totals = lax.psum(squares, 'din')]
    ppermute x5 -> x0, waiting for transfers between devices: 12.9 us -> none  [swapped(): return lax.ppermute(value, axis, pairs)]
    convert_element_type x4 -> x1, other arithmetic: 8.03 us -> 0.01 us  [shards(): angles = positions.astype(jnp.float32) * rotary_table(HD)]
  transfers between devices with their start and end apart: 8 -> 0, of which waited for: 7 -> 0; matrix products, arithmetic and copies ran while one was open for 2% -> 0% of each run, Pallas kernels for 0% -> 0%
where the time goes in v1:
time: 148 us
  Pallas kernels  141 us (95%)
  local copies, waits for them, and re-layouts  5.77 us (4%)
  other arithmetic  1.73 us (1%)
    pallas_call x1, Pallas kernels, shards(): pl.pallas_call(kernel, out_shape=jax.ShapeDtypeStruct((NB, ROWS_HERE * DR...  141 us
    unnamed x1, local copies, waits for them, and re-layouts  4.79 us

profile of v1, /device:TPU:0, one launch (start us, length us, event | category | flops | bytes accessed | tf_op | source)
XLA Modules:
  0.0 148.0 jit_solution(8780979246410248892)
XLA Ops:
  0.0 0.1 add.30
  0.1 0.7 add.26
  0.8 0.1 add.27
  0.9 0.1 add.28
  1.0 1.0 fusion
  2.0 0.8 pad_maximum_fusion
  2.7 140.5 %shard_map.118 = bf16[8,128,2048]{2,1,0:T(8,128)(2,1)} custom-call(s32[8]{0:T(128)} %lengths.1, f32[1,2048]{1,0:T(1,128)} %bitcast.8, f32[1,1024]{1,0:T(1,128)} %bitcast.10, f32[1,128]{1,0:T(1,128)} %bitcast.11, f32[1,2048]{1,0:T(1,128)} %bitcast.9, f32[4,32,128]{2,1,0:T(8,128)} %get-tuple-element.8.cosines, f32[4,32,128]{2,1,0:T(8,128)} %get-tuple-element.9.sines, ...), custom_call_target="tpu_custom_call" | custom-call | flops 12000000000 | bytes 26214400 | tf_op jit(solution)/shard_map/pallas_call | solution.py:505
  143.3 4.8 %copy.14 = bf16[1024,2048]{1,0:T(8,128)(2,1)} copy(bf16[1024,2048]{1,0:T(8,128)(2,1)} %bitcast.6) | data formatting | bytes 8388608
  (2 shorter events, 0.0 us)

commit v2 on v1

v2 whole, which is shorter than its diff:
```python
import functools
import math

import jax
import jax.numpy as jnp
from jax import lax
from jax.experimental import pallas as pl
from jax.experimental.pallas import tpu as pltpu
from jax.sharding import PartitionSpec as P

D = 16384
HQ = 128
KVH = 8
HD = 128
DRAFT = 16
ROWS_HERE = 8
OWN = 8
QW = OWN * HD
WIDE = QW + 2 * HD
SPAN = 2048
TILE = 512
FEATS = 2048
OUTS = 2048

CHUNK_ROWS = 2
NC = ROWS_HERE // CHUNK_ROWS
T = CHUNK_ROWS * DRAFT
NB = 8
M = NB * T
LOG_SCALE = math.log2(math.e) / math.sqrt(HD)
LOWEST = -1e30
LIMIT = 56

WIDTH = OUTS // 8

CORE = 0
ZRS = 1
SWAP = 7
FAR = 9
ZAG = FAR + CHUNK_ROWS
CAG = ZAG + 3
RS1 = CAG + 4
RS2 = RS1 + 12
AG2 = RS2 + 6
AG1 = AG2 + 6
NSEM = AG1 + 8

ORDER = (
    (0, 0), (1, 0), (0, 1), (3, 0), (1, 1), (0, 2), (2, 0), (1, 2), (2, 1), (0, 3),
    (1, 3), (2, 2), (3, 1), (0, 4), (2, 3), (3, 2), (1, 4), (0, 5), (3, 3), (2, 4),
    (1, 5), (0, 6), (3, 4), (0, 7), (2, 5), (1, 6), (1, 7), (3, 5), (2, 6), (0, 8),
    (1, 8), (2, 7), (3, 6), (0, 9), (3, 7), (2, 8), (1, 9), (0, 10), (3, 8), (2, 9),
    (1, 10), (0, 11), (3, 9), (1, 11), (2, 10), (3, 10), (1, 12), (2, 11), (1, 13), (3, 11),
    (2, 12), (0, 12), (3, 12), (0, 13), (2, 13), (3, 13),
)


def rotary_table(head_size):
    entries = []
    for index in range(head_size // 2):
        inverse = 1.0 / 500000.0 ** (2.0 * index / head_size)
        wavelength = 2.0 * math.pi / inverse
        smooth = min(max((8192.0 / wavelength - 1.0) / 3.0, 0.0), 1.0)
        entries.append((1.0 - smooth) * inverse / 8.0 + smooth * inverse)
    return jnp.asarray(entries, dtype=jnp.float32)


def mod4(v):
    return lax.rem(v, 4)


def f32(v):
    return v.astype(jnp.float32)


def kernel(
    lengths, frequencies, gain, qscale, kvscale, oscale,
    states, wq, wkv, wo, keys, values,
    out,
    cosines, sines,
    xs, wq_v, wkv_v, wo_v, k_v, v_v, scaled,
    ybuf, crecv, zrecv, qbuf, kvbuf, kpad, vpad, obuf, orecv, gat,
    pbuf,
    load_sem, send_sem, recv_sem,
    *sides,
):
    r1, gf, gb, r2 = (
        [[sides[4 * (2 * c + side) + kind] for side in range(2)] for c in range(NC)]
        for kind in range(4)
    )
    din = lax.axis_index("din")
    dout = lax.axis_index("dout")
    core = lax.rem(din, 2)
    z = lax.div(din, 2)
    x = lax.rem(dout, 4)
    y = lax.div(dout, 4)
    parity = lax.rem(x, 2)
    core_peer = (din + 1 - 2 * core, dout)
    pair_peer = (din, dout + 1 - 2 * parity)
    z_plus = (lax.rem(din + 2, 8), dout)
    z_minus = (lax.rem(din + 6, 8), dout)
    x_plus = (din, 4 * y + mod4(x + 1))
    x_minus = (din, 4 * y + mod4(x + 3))
    y_plus = (din, lax.rem(dout + 4, 16))
    y_minus = (din, lax.rem(dout + 12, 16))
    z_ring = (z_plus, (lax.rem(din + 4, 8), dout), z_minus)
    x_ring = (x_plus, (din, 4 * y + mod4(x + 2)), x_minus)
    y_ring = (y_plus, (din, lax.rem(dout + 8, 16)), y_minus)
    neighbours = (core_peer, *z_ring, *x_ring, *y_ring)

    def load(src, dst, index):
        return pltpu.make_async_copy(src, dst, load_sem.at[index])

    def states_load(c):
        return load(states.at[:, pl.ds(c * T, T), :], xs.at[c], c)

    wq_load = load(wq, wq_v, NC)
    wkv_load = load(wkv, wkv_v, NC + 1)
    wo_load = load(wo, wo_v, NC + 2)
    k_load = load(keys, k_v, NC + 3)
    v_load = load(values, v_v, NC + 4)
    states_load(0).start()
    wq_load.start()
    wkv_load.start()
    for c in range(1, NC):
        states_load(c).start()
    k_load.start()
    v_load.start()
    wo_load.start()

    draft = lax.broadcasted_iota(jnp.int32, (DRAFT, HD), 0)
    sign = jnp.where(lax.broadcasted_iota(jnp.int32, (DRAFT, HD), 1) < HD // 2, -1.0, 1.0)
    for row in range(ROWS_HERE):
        angles = f32(draft + lengths[row]) * frequencies[...]
        place = pl.ds(row * DRAFT, DRAFT)
        cosines[place] = jnp.cos(angles)
        sines[place] = jnp.sin(angles) * sign

    barrier = pltpu.get_barrier_semaphore()
    for peer in neighbours:
        pl.semaphore_signal(barrier, inc=1, device_id=peer, device_id_type=pl.DeviceIdType.MESH)
    pl.semaphore_wait(barrier, len(neighbours))

    started = []

    def remote(src, dst, row, c, peer):
        return pltpu.make_async_remote_copy(
            src_ref=src,
            dst_ref=dst,
            send_sem=send_sem.at[row, c],
            recv_sem=recv_sem.at[row, c],
            device_id=peer,
            device_id_type=pl.DeviceIdType.MESH,
        )

    def send(src, dst, row, c, peer):
        copy = remote(src, dst, row, c, peer)
        copy.start()
        started.append(copy)

    def arrived(dst, row, c):
        remote(dst, dst, row, c, core_peer).wait_recv()

    def scatter_start(base, c, shard, land, index, plus, minus):
        far = mod4(index + 2)
        send(shard(far, 1), land(0), base, c, plus)
        send(shard(far, 0), land(1), base + 1, c, minus)
        send(shard(mod4(index + 1), 0), land(2), base + 2, c, plus)
        send(shard(mod4(index + 3), 1), land(3), base + 3, c, minus)

    def scatter_mid(base, c, shard, land, index, plus, minus):
        for slot, step, half, peer in ((0, 1, 1, plus), (1, 3, 0, minus)):
            target = mod4(index + step)
            arrived(land(slot), base + slot, c)
            piece = shard(target, half)
            piece[...] = (f32(piece[...]) + f32(land(slot)[...])).astype(piece.dtype)
            send(piece, land(4 + slot), base + 4 + slot, c, peer)

    def to_ring(base, c, part, land, index, peers):
        for slot in (1, 0, 2):
            send(part(slot + 1), land(slot), base + slot, c, peers[slot])

    def scatter_end(base, c, shard, land, index):
        halves = []
        for half, direct, chained in ((0, 2, 5), (1, 3, 4)):
            arrived(land(direct), base + direct, c)
            arrived(land(chained), base + chained, c)
            halves.append(
                f32(shard(index, half)[...]) + f32(land(direct)[...]) + f32(land(chained)[...])
            )
        return halves

    def gather_start(base, c, part, index, plus, minus):
        own = part(index, None)
        send(own, own, base, c, plus)
        send(own, own, base + 1, c, minus)

    def gather_mid(base, c, part, index, plus, minus):
        for slot, step, half, peer in ((0, 3, 0, plus), (1, 1, 1, minus)):
            source = mod4(index + step)
            arrived(part(source, None), base + slot, c)
            piece = part(source, half)
            send(piece, piece, base + 2 + slot, c, peer)

    def gather_end(base, c, part, index):
        far = mod4(index + 2)
        arrived(part(far, 0), base + 2, c)
        arrived(part(far, 1), base + 3, c)

    def project(c):
        states_load(c).wait()
        wide = f32(xs[c]).reshape(M, FEATS)
        squares = jnp.sum(wide * wide, axis=1, keepdims=True)
        scaled[...] = (wide * gain[...]).astype(jnp.bfloat16)
        if c == 0:
            wq_load.wait()
            wkv_load.wait()

        def put(block, start):
            for b in range(NB):
                ybuf[c, b % 2, b // 2, :, start] = block[b * T : (b + 1) * T]

        put(jnp.broadcast_to(squares, (M, HD)), pl.ds(QW + HD, HD))
        put(
            jnp.dot(scaled[...], wkv_v[...], preferred_element_type=jnp.float32), pl.ds(QW, HD)
        )

        put(jnp.dot(scaled[...], wq_v[...], preferred_element_type=jnp.float32), pl.ds(0, QW))
        send(ybuf.at[c, 1 - core], crecv.at[c], CORE, c, core_peer)

    def z_shard(c):
        return lambda t, h: ybuf.at[c, core, t, pl.ds(h * (T // 2), T // 2), :]

    def z_land(c):
        return lambda slot: zrecv.at[c, slot]

    def pair_cores(c):
        arrived(crecv.at[c], CORE, c)
        ybuf[c, core] = ybuf[c, core] + crecv[c]
        scatter_start(ZRS, c, z_shard(c), z_land(c), z, z_plus, z_minus)

    def project_mid(c):
        scatter_mid(ZRS, c, z_shard(c), z_land(c), z, z_plus, z_minus)

    def project_end(c):
        total = jnp.concatenate(scatter_end(ZRS, c, z_shard(c), z_land(c), z), axis=0)
        inverse = lax.rsqrt(total[:, QW + HD :] / D + 1e-05)
        cosine = cosines[c * T : (c + 1) * T]
        sine = sines[c * T : (c + 1) * T]
        half = HD // 2
        for h in range(OWN):
            cols = slice(h * HD, (h + 1) * HD)
            raw = total[:, cols] * qscale[:, cols] * inverse
            turned = jnp.concatenate([raw[:, half:], raw[:, :half]], axis=1)
            query = (raw * cosine + turned * sine).astype(jnp.bfloat16)
            for r in range(CHUNK_ROWS):
                qbuf[c, parity, r, pl.ds(h * DRAFT, DRAFT), :] = query[
                    r * DRAFT : (r + 1) * DRAFT
                ]
        raw = total[:, QW : QW + HD] * kvscale[...] * inverse
        turned = jnp.concatenate([raw[:, half:], raw[:, :half]], axis=1)
        rotated = raw * cosine + turned * sine
        kvbuf[c, parity] = jnp.where(parity == 0, rotated, raw).astype(jnp.bfloat16)
        send(qbuf.at[c, parity], qbuf.at[c, parity], SWAP, c, pair_peer)
        send(kvbuf.at[c, parity], kvbuf.at[c, parity], SWAP + 1, c, pair_peer)

    def attend(c):
        if c == 0:
            kpad[...] = jnp.zeros_like(kpad)
            vpad[...] = jnp.zeros_like(vpad)
            k_load.wait()
            v_load.wait()
        arrived(qbuf.at[c, 1 - parity], SWAP, c)
        arrived(kvbuf.at[c, 1 - parity], SWAP + 1, c)
        place = lax.broadcasted_iota(jnp.int32, (1, SPAN), 1) + parity * SPAN
        token = lax.rem(lax.broadcasted_iota(jnp.int32, (2 * OWN * DRAFT, HD), 0), DRAFT)
        other = lax.broadcasted_iota(jnp.int32, (2 * OWN * DRAFT, HD), 1)
        drafted = (other <= token) & (parity == 0)
        lane = lax.broadcasted_iota(jnp.int32, (QW // OWN, HD), 1)
        for r in range(CHUNK_ROWS):
            row = c * CHUNK_ROWS + r
            kpad[r, 0:DRAFT] = kvbuf[c, 0, r * DRAFT : (r + 1) * DRAFT]
            vpad[r, 0:DRAFT] = kvbuf[c, 1, r * DRAFT : (r + 1) * DRAFT]
            query = jnp.concatenate([qbuf[c, 0, r], qbuf[c, 1, r]], axis=0)
            across = (((1,), (1,)), ((), ()))
            bias = jnp.where(place < lengths[row], 0.0, LOWEST)
            tiles = [slice(i * TILE, (i + 1) * TILE) for i in range(SPAN // TILE)]
            fresh = lax.dot_general(
                query, kpad[r], across, preferred_element_type=jnp.float32
            )
            fresh = jnp.where(drafted, fresh * LOG_SCALE, LOWEST)
            top = jnp.max(fresh, axis=1, keepdims=True)
            scores = []
            for tile in tiles:
                part = lax.dot_general(
                    query, k_v[row, tile], across, preferred_element_type=jnp.float32
                )
                scores.append(part * LOG_SCALE + bias[:, tile])
                top = jnp.maximum(top, jnp.max(scores[-1], axis=1, keepdims=True))
            weights = jnp.exp2(fresh - top)
            totals = jnp.sum(weights, axis=1, keepdims=True)
            weighted = jnp.dot(
                weights.astype(jnp.bfloat16), vpad[r], preferred_element_type=jnp.float32
            )
            for tile, part in zip(tiles, scores):
                weights = jnp.exp2(part - top)
                totals = totals + jnp.sum(weights, axis=1, keepdims=True)
                weighted = weighted + jnp.dot(
                    weights.astype(jnp.bfloat16), v_v[row, tile], preferred_element_type=jnp.float32
                )
            for p in range(2):
                mine = slice(p * QW // OWN, (p + 1) * QW // OWN)
                both = jnp.where(lane < HD // 2, top[mine], totals[mine]).T
                obuf[c, p, r, 0:HD] = weighted[mine]
                obuf[c, p, r, HD : HD + 8] = both[0:8]
                obuf[c, p, r, HD + 8 : HD + 16] = both[HD // 2 : HD // 2 + 8]
            send(obuf.at[c, 1 - parity, r], orecv.at[c, r], FAR + r, c, pair_peer)

    def to_core(c, slot, t):
        block = gat.at[c, 2 * t + core]
        send(block, block, CAG + slot, c, core_peer)

    def combine(c):
        for r in range(CHUNK_ROWS):
            arrived(orecv.at[c, r], FAR + r, c)
            near_top = obuf[c, parity, r, HD : HD + 8]
            near_total = obuf[c, parity, r, HD + 8 : HD + 16]
            far_top = orecv[c, r, HD : HD + 8]
            far_total = orecv[c, r, HD + 8 : HD + 16]
            joint = jnp.maximum(near_top, far_top)
            near_factor = jnp.exp2(near_top - joint)
            far_factor = jnp.exp2(far_top - joint)
            share = 1.0 / (near_total * near_factor + far_total * far_factor)

            def spread(factor):
                return jnp.broadcast_to((factor * share)[0:1], (HD, HD)).T

            heads = (
                obuf[c, parity, r, 0:HD] * spread(near_factor)
                + orecv[c, r, 0:HD] * spread(far_factor)
            ).astype(jnp.bfloat16)
            for h in range(OWN):
                gat[c, din, r * DRAFT : (r + 1) * DRAFT, h * HD : (h + 1) * HD] = heads[
                    h * DRAFT : (h + 1) * DRAFT
                ]
        own = gat.at[c, din]
        to_ring(ZAG, c, lambda step: own, lambda slot: own, z, z_ring)
        to_core(c, 3, z)

    def gather_heads(c):
        for slot in (0, 2, 1):
            t = mod4(z + 3 - slot)
            arrived(gat.at[c, 2 * t + core], ZAG + slot, c)
            to_core(c, slot, t)

    first = ((x, x_plus, x_minus), (y, y_plus, y_minus))
    second = ((y, y_ring), (x, x_ring))

    def columns(side, t):
        return pl.ds(pl.multiple_of((4 * side + t) * WIDTH, WIDTH), WIDTH)

    def rows(c):
        return pl.ds(c * T, T)

    def shard1(c, side):
        return lambda t, h: pbuf.at[c, pl.ds(h * 4, 4), :, columns(side, t)]

    def land1(c, side):
        return lambda slot: r1[c][side].at[slot]

    def part2(c, side, t):
        return out.at[pl.ds(2 * t, 2), rows(c), columns(side, first[side][0])]

    def part1(c, side):
        def part(t, half):
            if half is None:
                return out.at[:, rows(c), columns(side, t)]
            return out.at[pl.ds(half * 4, 4), rows(c), columns(side, t)]

        return part

    def output(c):
        if c == 0:
            wo_load.wait()
        for slot in (3, 0, 2, 1):
            t = mod4(z + 3 - slot)
            arrived(gat.at[c, 2 * t + 1 - core], CAG + slot, c)

        heads = gat[c].reshape(M, QW)
        for side in range(2):
            width = OUTS // 2
            cols = slice(side * width, (side + 1) * width)
            block = jnp.dot(heads, wo_v[:, cols], preferred_element_type=jnp.float32)
            pbuf[c, :, :, cols] = block.astype(jnp.bfloat16).reshape(NB, T, width)
            scatter_start(RS1 + 6 * side, c, shard1(c, side), land1(c, side), *first[side])

    def sum_mid(c):
        for side in range(2):
            scatter_mid(RS1 + 6 * side, c, shard1(c, side), land1(c, side), *first[side])

    def sum_end(c):
        for side in range(2):
            halves = scatter_end(
                RS1 + 6 * side, c, shard1(c, side), land1(c, side), first[side][0]
            )
            for h in range(2):
                gf[c][side][h * 4 : (h + 1) * 4] = halves[h]
                gb[c][side][h * 4 : (h + 1) * 4] = halves[h].astype(jnp.bfloat16)
            index, ring = second[side]
            to_ring(
                RS2 + 3 * side,
                c,
                lambda step: gb[c][side].at[pl.ds(2 * mod4(index + step), 2)],
                lambda slot: r2[c][side].at[slot],
                index,
                ring,
            )

    def cross_end(c):
        for side in range(2):
            index, ring = second[side]
            total = gf[c][side][pl.ds(2 * index, 2)]
            for slot in range(3):
                arrived(r2[c][side].at[slot], RS2 + 3 * side + slot, c)
                total = total + f32(r2[c][side][slot])
            cols = columns(side, first[side][0])
            part2(c, side, index)[...] = (total * oscale[:, cols]).astype(jnp.bfloat16)
            own = part2(c, side, index)
            to_ring(AG2 + 3 * side, c, lambda step: own, lambda slot: own, index, ring)

    def spread_end(c):
        for side in range(2):
            index, _ = second[side]
            for slot in range(3):
                arrived(part2(c, side, mod4(index + 3 - slot)), AG2 + 3 * side + slot, c)
            gather_start(AG1 + 4 * side, c, part1(c, side), *first[side])

    def last_mid(c):
        for side in range(2):
            gather_mid(AG1 + 4 * side, c, part1(c, side), *first[side])

    def last_end(c):
        for side in range(2):
            gather_end(AG1 + 4 * side, c, part1(c, side), first[side][0])

    stages = (
        project,
        pair_cores,
        project_mid,
        project_end,
        attend,
        combine,
        gather_heads,
        output,
        sum_mid,
        sum_end,
        cross_end,
        spread_end,
        last_mid,
        last_end,
    )
    for c, i in ORDER:
        stages[i](c)

    for copy in started:
        copy.wait_send()


def shards(
    states,
    lengths,
    norm_gain,
    query_weight,
    keyval_weight,
    output_weight,
    query_scale,
    keyval_scale,
    output_scale,
    key_cache,
    value_cache,
):
    table = rotary_table(HD)
    frequencies = jnp.concatenate([table, table])[None, :]
    bf16 = jnp.bfloat16
    vmem = pl.BlockSpec(memory_space=pltpu.VMEM)
    smem = pl.BlockSpec(memory_space=pltpu.SMEM)
    hbm = pl.BlockSpec(memory_space=pl.ANY)
    result = pl.pallas_call(
        kernel,
        out_shape=pltpu.VMEM((NB, ROWS_HERE * DRAFT, OUTS), bf16),
        in_specs=[smem] + [vmem] * 5 + [hbm] * 6,
        out_specs=vmem,
        scratch_shapes=[
            pltpu.VMEM((ROWS_HERE * DRAFT, HD), jnp.float32),
            pltpu.VMEM((ROWS_HERE * DRAFT, HD), jnp.float32),
            pltpu.VMEM((NC, NB, T, FEATS), bf16),
            pltpu.VMEM((FEATS, QW), bf16),
            pltpu.VMEM((FEATS, HD), bf16),
            pltpu.VMEM((QW, OUTS), bf16),
            pltpu.VMEM((ROWS_HERE, SPAN, HD), bf16),
            pltpu.VMEM((ROWS_HERE, SPAN, HD), bf16),
            pltpu.VMEM((M, FEATS), bf16),
            pltpu.VMEM((NC, 2, 4, T, WIDE), jnp.float32),
            pltpu.VMEM((NC, 4, T, WIDE), jnp.float32),
            pltpu.VMEM((NC, 6, T // 2, WIDE), jnp.float32),
            pltpu.VMEM((NC, 2, CHUNK_ROWS, OWN * DRAFT, HD), bf16),
            pltpu.VMEM((NC, 2, T, HD), bf16),
            pltpu.VMEM((CHUNK_ROWS, HD, HD), bf16),
            pltpu.VMEM((CHUNK_ROWS, HD, HD), bf16),
            pltpu.VMEM((NC, 2, CHUNK_ROWS, HD + 16, HD), jnp.float32),
            pltpu.VMEM((NC, CHUNK_ROWS, HD + 16, HD), jnp.float32),
            pltpu.VMEM((NC, NB, T, QW), bf16),
            pltpu.VMEM((NC, NB, T, OUTS), bf16),
            pltpu.SemaphoreType.DMA((NC + 5,)),
            pltpu.SemaphoreType.DMA((NSEM, NC)),
            pltpu.SemaphoreType.DMA((NSEM, NC)),
            *(
                shape
                for c in range(NC)
                for _ in range(2)
                for shape in (
                    pltpu.VMEM((6, 4, T, WIDTH), bf16),
                    pltpu.VMEM((NB, T, WIDTH), jnp.float32),
                    pltpu.VMEM((NB, T, WIDTH), bf16),
                    pltpu.VMEM((3, 2, T, WIDTH), bf16),
                )
            ),
        ],
        compiler_params=pltpu.CompilerParams(
            collective_id=0, has_side_effects=True, vmem_limit_bytes=LIMIT * 2**20
        ),
        cost_estimate=pl.CostEstimate(
            flops=12 * 10**9, bytes_accessed=25 * 2**20, transcendentals=2**22
        ),
    )(
        lengths,
        frequencies,
        norm_gain[None, :],
        query_scale[None, :],
        keyval_scale[None, :],
        output_scale[None, :],
        states.reshape(NB, ROWS_HERE * DRAFT, FEATS),
        query_weight,
        keyval_weight,
        output_weight,
        key_cache,
        value_cache,
    )
    return result.reshape(NB * ROWS_HERE * DRAFT, OUTS)


def solution(mesh):
    placed = (
        P(None, "din"),
        P("din"),
        P("din"),
        P("din", "dout"),
        P("din", "dout"),
        P("dout", "din"),
        P("dout"),
        P("dout"),
        P("din"),
        P("din", "dout", None),
        P("din", "dout", None),
    )
    return jax.shard_map(
        shards, mesh=mesh, in_specs=placed, out_specs=P(None, "din"), check_vma=False
    )
```

time: 148 us -> 98.5 us (0.67)
  Pallas kernels: 141 us -> 96.3 us
  local copies, waits for them, and re-layouts: 5.77 us -> 2.02 us
  other arithmetic: 1.73 us -> 0 us
    pallas_call x1, Pallas kernels: 141 us -> 96.3 us  [shards(): pl.pallas_call(kernel, out_shape=pltpu.VMEM((NB, ROWS_HERE * DRAFT, OUTS)...]
    unnamed x1, local copies, waits for them, and re-layouts: 4.79 us -> 2.02 us
where the time goes in v2:
time: 98.5 us; the launch traced here: 98.3 us
  Pallas kernels  96.3 us (98%)
  local copies, waits for them, and re-layouts  2.02 us (2%)
    pallas_call x1, Pallas kernels, shards(): pl.pallas_call(kernel, out_shape=pltpu.VMEM((NB, ROWS_HERE * DRAFT, OUTS)...  96.3 us
    unnamed x1, local copies, waits for them, and re-layouts  2.02 us

profile of v2, /device:TPU:0, one launch (start us, length us, event | category | flops | bytes accessed | tf_op | source)
XLA Modules:
  0.0 98.3 jit_solution(6734097093077853496)
XLA Ops:
  0.0 96.3 %shard_map.118 = bf16[8,128,2048]{2,1,0:T(8,128)(2,1)S(1)} custom-call(s32[8]{0:T(128)} %lengths.1, f32[1,128]{1,0:T(1,128)} %constant.4.frequencies, f32[1,2048]{1,0:T(1,128)} %bitcast.8, f32[1,1024]{1,0:T(1,128)} %bitcast.10, f32[1,128]{1,0:T(1,128)} %bitcast.11, f32[1,2048]{1,0:T(1,128)} %bitcast.9, bf16[8,128,2048]{2,1,0:T(8,128)(2,1)} %bitcast.7, ...), custom_call_target="tpu_custom_call" | custom-call | flops 12000000000 | bytes 26214400 | tf_op jit(solution)/shard_map/pallas_call | solution.py:488
  96.3 2.0 %copy.14 = bf16[1024,2048]{1,0:T(8,128)(2,1)} copy(bf16[1024,2048]{1,0:T(8,128)(2,1)S(1)} %bitcast.6) | data formatting | bytes 8388608

commit v3 on v2

--- a/solution.py
+++ b/solution.py
@@ -22,7 +22,7 @@
 FEATS = 2048
 OUTS = 2048
 
-CHUNK_ROWS = 2
+CHUNK_ROWS = 1
 NC = ROWS_HERE // CHUNK_ROWS
 T = CHUNK_ROWS * DRAFT
 NB = 8
@@ -35,23 +35,33 @@
 
 CORE = 0
 ZRS = 1
-SWAP = 7
-FAR = 9
-ZAG = FAR + CHUNK_ROWS
+SWAP = 3
+FAR = 5
+TOPS = FAR + CHUNK_ROWS
+ZAG = TOPS + CHUNK_ROWS
 CAG = ZAG + 3
-RS1 = CAG + 4
-RS2 = RS1 + 12
-AG2 = RS2 + 6
-AG1 = AG2 + 6
-NSEM = AG1 + 8
+RS1 = CAG + 1
+RS2 = RS1 + 4
+AG2 = RS2 + 2
+AG1 = AG2 + 2
+ARRIVALS = AG1 + 4
+CORE_OUT, ZRS_OUT, SWAP_OUT, FAR_OUT, ZAG_OUT, CAG_OUT = 0, 1, 2, 4, 5, 6
+RS1_OUT, RS2_OUT, AG2_OUT, AG1_OUT, TOPS_OUT = 7, 9, 11, 13, 15
+DEPARTURES = 16
 
 ORDER = (
-    (0, 0), (1, 0), (0, 1), (3, 0), (1, 1), (0, 2), (2, 0), (1, 2), (2, 1), (0, 3),
-    (1, 3), (2, 2), (3, 1), (0, 4), (2, 3), (3, 2), (1, 4), (0, 5), (3, 3), (2, 4),
-    (1, 5), (0, 6), (3, 4), (0, 7), (2, 5), (1, 6), (1, 7), (3, 5), (2, 6), (0, 8),
-    (1, 8), (2, 7), (3, 6), (0, 9), (3, 7), (2, 8), (1, 9), (0, 10), (3, 8), (2, 9),
-    (1, 10), (0, 11), (3, 9), (1, 11), (2, 10), (3, 10), (1, 12), (2, 11), (1, 13), (3, 11),
-    (2, 12), (0, 12), (3, 12), (0, 13), (2, 13), (3, 13),
+    (0, 0), (1, 0), (0, 1), (4, 0), (1, 1), (4, 1), (0, 2), (5, 0), (3, 0), (1, 2),
+    (6, 0), (3, 1), (2, 0), (6, 1), (2, 1), (1, 3), (3, 2), (0, 3), (7, 0), (5, 1),
+    (2, 2), (4, 2), (0, 4), (1, 4), (3, 3), (7, 1), (5, 2), (2, 3), (6, 2), (4, 3),
+    (0, 5), (7, 2), (3, 4), (5, 3), (1, 5), (2, 4), (6, 3), (0, 6), (4, 4), (7, 3),
+    (3, 5), (0, 7), (1, 6), (2, 5), (5, 4), (1, 7), (6, 4), (4, 5), (3, 6), (7, 4),
+    (0, 8), (2, 6), (1, 8), (2, 7), (3, 7), (7, 5), (5, 5), (6, 5), (0, 9), (4, 6),
+    (1, 9), (2, 8), (4, 7), (3, 8), (7, 6), (0, 10), (7, 7), (5, 6), (1, 10), (4, 8),
+    (6, 6), (5, 7), (6, 7), (7, 8), (3, 9), (4, 9), (1, 11), (5, 8), (7, 9), (2, 9),
+    (6, 8), (0, 11), (4, 10), (3, 10), (5, 9), (6, 9), (2, 10), (1, 12), (7, 10), (0, 12),
+    (5, 10), (4, 11), (6, 10), (3, 11), (5, 11), (2, 11), (7, 11), (6, 11), (1, 13), (4, 12),
+    (2, 12), (3, 12), (5, 12), (7, 12), (6, 12), (4, 13), (2, 13), (0, 13), (7, 13), (5, 13),
+    (3, 13), (6, 13),
 )
 
 
@@ -79,7 +89,7 @@
     out,
     cosines, sines,
     xs, wq_v, wkv_v, wo_v, k_v, v_v, scaled,
-    ybuf, crecv, zrecv, qbuf, kvbuf, kpad, vpad, obuf, orecv, gat,
+    ybuf, crecv, zrecv, qbuf, kvbuf, kpad, vpad, obuf, osend, orecv, tops, trecv, gat,
     pbuf,
     load_sem, send_sem, recv_sem,
     *sides,
@@ -128,6 +138,9 @@
     v_load.start()
     wo_load.start()
 
+    barrier = pltpu.get_barrier_semaphore()
+    for peer in neighbours:
+        pl.semaphore_signal(barrier, inc=1, device_id=peer, device_id_type=pl.DeviceIdType.MESH)
     draft = lax.broadcasted_iota(jnp.int32, (DRAFT, HD), 0)
     sign = jnp.where(lax.broadcasted_iota(jnp.int32, (DRAFT, HD), 1) < HD // 2, -1.0, 1.0)
     for row in range(ROWS_HERE):
@@ -135,77 +148,65 @@
         place = pl.ds(row * DRAFT, DRAFT)
         cosines[place] = jnp.cos(angles)
         sines[place] = jnp.sin(angles) * sign
-
-    barrier = pltpu.get_barrier_semaphore()
-    for peer in neighbours:
-        pl.semaphore_signal(barrier, inc=1, device_id=peer, device_id_type=pl.DeviceIdType.MESH)
     pl.semaphore_wait(barrier, len(neighbours))
 
-    started = []
-
-    def remote(src, dst, row, c, peer):
+    def remote(src, dst, out_row, row, c, peer):
         return pltpu.make_async_remote_copy(
             src_ref=src,
             dst_ref=dst,
-            send_sem=send_sem.at[row, c],
+            send_sem=send_sem.at[out_row, c],
             recv_sem=recv_sem.at[row, c],
             device_id=peer,
             device_id_type=pl.DeviceIdType.MESH,
         )
 
-    def send(src, dst, row, c, peer):
-        copy = remote(src, dst, row, c, peer)
-        copy.start()
-        started.append(copy)
-
-    def arrived(dst, row, c):
-        remote(dst, dst, row, c, core_peer).wait_recv()
-
-    def scatter_start(base, c, shard, land, index, plus, minus):
+    def send(src, dst, out_row, row, c, peer):
+        remote(src, dst, out_row, row, c, peer).start()
+
+    def arrived(like, row, c):
+        remote(like, like, 0, row, c, core_peer).wait_recv()
+
+    def departed(like, out_row, c):
+        remote(like, like, out_row, 0, c, core_peer).wait_send()
+
+    def scatter_start(out_row, row, c, shard, land, index, plus, minus):
         far = mod4(index + 2)
-        send(shard(far, 1), land(0), base, c, plus)
-        send(shard(far, 0), land(1), base + 1, c, minus)
-        send(shard(mod4(index + 1), 0), land(2), base + 2, c, plus)
-        send(shard(mod4(index + 3), 1), land(3), base + 3, c, minus)
-
-    def scatter_mid(base, c, shard, land, index, plus, minus):
+        send(shard(far, 1), land.at[0], out_row, row, c, plus)
+        send(shard(far, 0), land.at[1], out_row, row, c, minus)
+        send(shard(mod4(index + 1), 0), land.at[2], out_row, row + 1, c, plus)
+        send(shard(mod4(index + 3), 1), land.at[3], out_row, row + 1, c, minus)
+
+    def scatter_mid(out_row, row, c, shard, land, index, plus, minus):
+        arrived(land.at[pl.ds(0, 2)], row, c)
         for slot, step, half, peer in ((0, 1, 1, plus), (1, 3, 0, minus)):
-            target = mod4(index + step)
-            arrived(land(slot), base + slot, c)
-            piece = shard(target, half)
-            piece[...] = (f32(piece[...]) + f32(land(slot)[...])).astype(piece.dtype)
-            send(piece, land(4 + slot), base + 4 + slot, c, peer)
-
-    def to_ring(base, c, part, land, index, peers):
+            piece = shard(mod4(index + step), half)
+            piece[...] = (f32(piece[...]) + f32(land[slot])).astype(piece.dtype)
+            send(piece, land.at[4 + slot], out_row, row + 1, c, peer)
+
+    def to_ring(out_row, rows, c, part, land, index, peers):
         for slot in (1, 0, 2):
-            send(part(slot + 1), land(slot), base + slot, c, peers[slot])
-
-    def scatter_end(base, c, shard, land, index):
-        halves = []
-        for half, direct, chained in ((0, 2, 5), (1, 3, 4)):
-            arrived(land(direct), base + direct, c)
-            arrived(land(chained), base + chained, c)
-            halves.append(
-                f32(shard(index, half)[...]) + f32(land(direct)[...]) + f32(land(chained)[...])
-            )
-        return halves
-
-    def gather_start(base, c, part, index, plus, minus):
+            send(part(slot + 1), land(slot), out_row, rows[slot], c, peers[slot])
+
+    def scatter_end(row, c, shard, land, index):
+        arrived(land.at[pl.ds(2, 4)], row + 1, c)
+        return [
+            f32(shard(index, half)[...]) + f32(land[direct]) + f32(land[chained])
+            for half, direct, chained in ((0, 2, 5), (1, 3, 4))
+        ]
+
+    def gather_start(out_row, row, c, part, index, plus, minus):
         own = part(index, None)
-        send(own, own, base, c, plus)
-        send(own, own, base + 1, c, minus)
-
-    def gather_mid(base, c, part, index, plus, minus):
-        for slot, step, half, peer in ((0, 3, 0, plus), (1, 1, 1, minus)):
-            source = mod4(index + step)
-            arrived(part(source, None), base + slot, c)
-            piece = part(source, half)
-            send(piece, piece, base + 2 + slot, c, peer)
-
-    def gather_end(base, c, part, index):
-        far = mod4(index + 2)
-        arrived(part(far, 0), base + 2, c)
-        arrived(part(far, 1), base + 3, c)
+        send(own, own, out_row, row, c, plus)
+        send(own, own, out_row, row, c, minus)
+
+    def gather_mid(out_row, row, c, part, like, index, plus, minus):
+        arrived(like.at[pl.ds(0, 4)], row, c)
+        for step, half, peer in ((3, 0, plus), (1, 1, minus)):
+            piece = part(mod4(index + step), half)
+            send(piece, piece, out_row, row + 1, c, peer)
+
+    def gather_end(row, c, like):
+        arrived(like.at[pl.ds(0, 2)], row + 1, c)
 
     def project(c):
         states_load(c).wait()
@@ -226,24 +227,21 @@
         )
 
         put(jnp.dot(scaled[...], wq_v[...], preferred_element_type=jnp.float32), pl.ds(0, QW))
-        send(ybuf.at[c, 1 - core], crecv.at[c], CORE, c, core_peer)
+        send(ybuf.at[c, 1 - core], crecv.at[c], CORE_OUT, CORE, c, core_peer)
 
     def z_shard(c):
         return lambda t, h: ybuf.at[c, core, t, pl.ds(h * (T // 2), T // 2), :]
-
-    def z_land(c):
-        return lambda slot: zrecv.at[c, slot]
 
     def pair_cores(c):
         arrived(crecv.at[c], CORE, c)
         ybuf[c, core] = ybuf[c, core] + crecv[c]
-        scatter_start(ZRS, c, z_shard(c), z_land(c), z, z_plus, z_minus)
+        scatter_start(ZRS_OUT, ZRS, c, z_shard(c), zrecv.at[c], z, z_plus, z_minus)
 
     def project_mid(c):
-        scatter_mid(ZRS, c, z_shard(c), z_land(c), z, z_plus, z_minus)
+        scatter_mid(ZRS_OUT, ZRS, c, z_shard(c), zrecv.at[c], z, z_plus, z_minus)
 
     def project_end(c):
-        total = jnp.concatenate(scatter_end(ZRS, c, z_shard(c), z_land(c), z), axis=0)
+        total = jnp.concatenate(scatter_end(ZRS, c, z_shard(c), zrecv.at[c], z), axis=0)
         inverse = lax.rsqrt(total[:, QW + HD :] / D + 1e-05)
         cosine = cosines[c * T : (c + 1) * T]
         sine = sines[c * T : (c + 1) * T]
@@ -261,8 +259,8 @@
         turned = jnp.concatenate([raw[:, half:], raw[:, :half]], axis=1)
         rotated = raw * cosine + turned * sine
         kvbuf[c, parity] = jnp.where(parity == 0, rotated, raw).astype(jnp.bfloat16)
-        send(qbuf.at[c, parity], qbuf.at[c, parity], SWAP, c, pair_peer)
-        send(kvbuf.at[c, parity], kvbuf.at[c, parity], SWAP + 1, c, pair_peer)
+        send(qbuf.at[c, parity], qbuf.at[c, parity], SWAP_OUT, SWAP, c, pair_peer)
+        send(kvbuf.at[c, parity], kvbuf.at[c, parity], SWAP_OUT + 1, SWAP + 1, c, pair_peer)
 
     def attend(c):
         if c == 0:
@@ -311,22 +309,24 @@
             for p in range(2):
                 mine = slice(p * QW // OWN, (p + 1) * QW // OWN)
                 both = jnp.where(lane < HD // 2, top[mine], totals[mine]).T
-                obuf[c, p, r, 0:HD] = weighted[mine]
-                obuf[c, p, r, HD : HD + 8] = both[0:8]
-                obuf[c, p, r, HD + 8 : HD + 16] = both[HD // 2 : HD // 2 + 8]
-            send(obuf.at[c, 1 - parity, r], orecv.at[c, r], FAR + r, c, pair_peer)
-
-    def to_core(c, slot, t):
+                obuf[c, p, r] = weighted[mine]
+                osend[c, p, r] = weighted[mine].astype(jnp.bfloat16)
+                tops[c, p, r, 0:4] = both[0:4]
+                tops[c, p, r, 4:8] = both[HD // 2 : HD // 2 + 4]
+            far = 1 - parity
+            send(tops.at[c, far, r], trecv.at[c, r], TOPS_OUT, TOPS + r, c, pair_peer)
+            send(osend.at[c, far, r], orecv.at[c, r], FAR_OUT, FAR + r, c, pair_peer)
+
+    def to_core(c, t):
         block = gat.at[c, 2 * t + core]
-        send(block, block, CAG + slot, c, core_peer)
+        send(block, block, CAG_OUT, CAG, c, core_peer)
 
     def combine(c):
         for r in range(CHUNK_ROWS):
+            arrived(trecv.at[c, r], TOPS + r, c)
             arrived(orecv.at[c, r], FAR + r, c)
-            near_top = obuf[c, parity, r, HD : HD + 8]
-            near_total = obuf[c, parity, r, HD + 8 : HD + 16]
-            far_top = orecv[c, r, HD : HD + 8]
-            far_total = orecv[c, r, HD + 8 : HD + 16]
+            near_top, near_total = tops[c, parity, r, 0:4], tops[c, parity, r, 4:8]
+            far_top, far_total = trecv[c, r, 0:4], trecv[c, r, 4:8]
             joint = jnp.maximum(near_top, far_top)
             near_factor = jnp.exp2(near_top - joint)
             far_factor = jnp.exp2(far_top - joint)
@@ -336,22 +336,23 @@
                 return jnp.broadcast_to((factor * share)[0:1], (HD, HD)).T
 
             heads = (
-                obuf[c, parity, r, 0:HD] * spread(near_factor)
-                + orecv[c, r, 0:HD] * spread(far_factor)
+                obuf[c, parity, r] * spread(near_factor)
+                + f32(orecv[c, r]) * spread(far_factor)
             ).astype(jnp.bfloat16)
             for h in range(OWN):
                 gat[c, din, r * DRAFT : (r + 1) * DRAFT, h * HD : (h + 1) * HD] = heads[
                     h * DRAFT : (h + 1) * DRAFT
                 ]
         own = gat.at[c, din]
-        to_ring(ZAG, c, lambda step: own, lambda slot: own, z, z_ring)
-        to_core(c, 3, z)
+        rows = (ZAG, ZAG + 1, ZAG + 2)
+        to_ring(ZAG_OUT, rows, c, lambda step: own, lambda slot: own, z, z_ring)
+        to_core(c, z)
 
     def gather_heads(c):
         for slot in (0, 2, 1):
             t = mod4(z + 3 - slot)
             arrived(gat.at[c, 2 * t + core], ZAG + slot, c)
-            to_core(c, slot, t)
+            to_core(c, t)
 
     first = ((x, x_plus, x_minus), (y, y_plus, y_minus))
     second = ((y, y_ring), (x, x_ring))
@@ -364,9 +365,6 @@
 
     def shard1(c, side):
         return lambda t, h: pbuf.at[c, pl.ds(h * 4, 4), :, columns(side, t)]
-
-    def land1(c, side):
-        return lambda slot: r1[c][side].at[slot]
 
     def part2(c, side, t):
         return out.at[pl.ds(2 * t, 2), rows(c), columns(side, first[side][0])]
@@ -382,9 +380,7 @@
     def output(c):
         if c == 0:
             wo_load.wait()
-        for slot in (3, 0, 2, 1):
-            t = mod4(z + 3 - slot)
-            arrived(gat.at[c, 2 * t + 1 - core], CAG + slot, c)
+        arrived(gat.at[c, pl.ds(0, 4)], CAG, c)
 
         heads = gat[c].reshape(M, QW)
         for side in range(2):
@@ -392,23 +388,26 @@
             cols = slice(side * width, (side + 1) * width)
             block = jnp.dot(heads, wo_v[:, cols], preferred_element_type=jnp.float32)
             pbuf[c, :, :, cols] = block.astype(jnp.bfloat16).reshape(NB, T, width)
-            scatter_start(RS1 + 6 * side, c, shard1(c, side), land1(c, side), *first[side])
+            sums = (c, shard1(c, side), r1[c][side], *first[side])
+            scatter_start(RS1_OUT + side, RS1 + 2 * side, *sums)
 
     def sum_mid(c):
         for side in range(2):
-            scatter_mid(RS1 + 6 * side, c, shard1(c, side), land1(c, side), *first[side])
+            sums = (c, shard1(c, side), r1[c][side], *first[side])
+            scatter_mid(RS1_OUT + side, RS1 + 2 * side, *sums)
 
     def sum_end(c):
         for side in range(2):
             halves = scatter_end(
-                RS1 + 6 * side, c, shard1(c, side), land1(c, side), first[side][0]
+                RS1 + 2 * side, c, shard1(c, side), r1[c][side], first[side][0]
             )
             for h in range(2):
                 gf[c][side][h * 4 : (h + 1) * 4] = halves[h]
                 gb[c][side][h * 4 : (h + 1) * 4] = halves[h].astype(jnp.bfloat16)
             index, ring = second[side]
             to_ring(
-                RS2 + 3 * side,
+                RS2_OUT + side,
+                (RS2 + side,) * 3,
                 c,
                 lambda step: gb[c][side].at[pl.ds(2 * mod4(index + step), 2)],
                 lambda slot: r2[c][side].at[slot],
@@ -420,28 +419,35 @@
         for side in range(2):
             index, ring = second[side]
             total = gf[c][side][pl.ds(2 * index, 2)]
+            arrived(r2[c][side], RS2 + side, c)
             for slot in range(3):
-                arrived(r2[c][side].at[slot], RS2 + 3 * side + slot, c)
                 total = total + f32(r2[c][side][slot])
             cols = columns(side, first[side][0])
             part2(c, side, index)[...] = (total * oscale[:, cols]).astype(jnp.bfloat16)
             own = part2(c, side, index)
-            to_ring(AG2 + 3 * side, c, lambda step: own, lambda slot: own, index, ring)
+            to_ring(
+                AG2_OUT + side,
+                (AG2 + side,) * 3,
+                c,
+                lambda step: own,
+                lambda slot: own,
+                index,
+                ring,
+            )
 
     def spread_end(c):
         for side in range(2):
-            index, _ = second[side]
-            for slot in range(3):
-                arrived(part2(c, side, mod4(index + 3 - slot)), AG2 + 3 * side + slot, c)
-            gather_start(AG1 + 4 * side, c, part1(c, side), *first[side])
+            arrived(r2[c][side], AG2 + side, c)
+            gather_start(AG1_OUT + side, AG1 + 2 * side, c, part1(c, side), *first[side])
 
     def last_mid(c):
         for side in range(2):
-            gather_mid(AG1 + 4 * side, c, part1(c, side), *first[side])
+            spread = (c, part1(c, side), r1[c][side], *first[side])
+            gather_mid(AG1_OUT + side, AG1 + 2 * side, *spread)
 
     def last_end(c):
         for side in range(2):
-            gather_end(AG1 + 4 * side, c, part1(c, side), first[side][0])
+            gather_end(AG1 + 2 * side, c, r1[c][side])
 
     stages = (
         project,
@@ -462,8 +468,20 @@
     for c, i in ORDER:
         stages[i](c)
 
-    for copy in started:
-        copy.wait_send()
+    for c in range(NC):
+        departed(crecv.at[c], CORE_OUT, c)
+        departed(zrecv.at[c], ZRS_OUT, c)
+        departed(qbuf.at[c, 0], SWAP_OUT, c)
+        departed(kvbuf.at[c, 0], SWAP_OUT + 1, c)
+        departed(orecv.at[c], FAR_OUT, c)
+        departed(trecv.at[c], TOPS_OUT, c)
+        departed(gat.at[c, pl.ds(0, 3)], ZAG_OUT, c)
+        departed(gat.at[c, pl.ds(0, 4)], CAG_OUT, c)
+        for side in range(2):
+            departed(r1[c][side], RS1_OUT + side, c)
+            departed(r2[c][side], RS2_OUT + side, c)
+            departed(r2[c][side], AG2_OUT + side, c)
+            departed(r1[c][side], AG1_OUT + side, c)
 
 
 def shards(
@@ -507,13 +525,16 @@
             pltpu.VMEM((NC, 2, T, HD), bf16),
             pltpu.VMEM((CHUNK_ROWS, HD, HD), bf16),
             pltpu.VMEM((CHUNK_ROWS, HD, HD), bf16),
-            pltpu.VMEM((NC, 2, CHUNK_ROWS, HD + 16, HD), jnp.float32),
-            pltpu.VMEM((NC, CHUNK_ROWS, HD + 16, HD), jnp.float32),
+            pltpu.VMEM((NC, 2, CHUNK_ROWS, HD, HD), jnp.float32),
+            pltpu.VMEM((NC, 2, CHUNK_ROWS, HD, HD), bf16),
+            pltpu.VMEM((NC, CHUNK_ROWS, HD, HD), bf16),
+            pltpu.VMEM((NC, 2, CHUNK_ROWS, 8, HD), jnp.float32),
+            pltpu.VMEM((NC, CHUNK_ROWS, 8, HD), jnp.float32),
             pltpu.VMEM((NC, NB, T, QW), bf16),
             pltpu.VMEM((NC, NB, T, OUTS), bf16),
             pltpu.SemaphoreType.DMA((NC + 5,)),
-            pltpu.SemaphoreType.DMA((NSEM, NC)),
-            pltpu.SemaphoreType.DMA((NSEM, NC)),
+            pltpu.SemaphoreType.DMA((DEPARTURES, NC)),
+            pltpu.SemaphoreType.DMA((ARRIVALS, NC)),
             *(
                 shape
                 for c in range(NC)

time: 98.5 us -> 93.3 us (0.947)
  Pallas kernels: 96.3 us -> 90.9 us
    pallas_call x1, Pallas kernels: 96.3 us -> 90.9 us  [shards(): pl.pallas_call(kernel, out_shape=pltpu.VMEM((NB, ROWS_HERE * DRAFT, OUTS)...]
where the time goes in v3:
time: 93.3 us; the launch traced here: 92.9 us
  Pallas kernels  90.9 us (97%)
  local copies, waits for them, and re-layouts  2.02 us (2%)
    pallas_call x1, Pallas kernels, shards(): pl.pallas_call(kernel, out_shape=pltpu.VMEM((NB, ROWS_HERE * DRAFT, OUTS)...  90.9 us
    unnamed x1, local copies, waits for them, and re-layouts  2.02 us

profile of v3, /device:TPU:0, one launch (start us, length us, event | category | flops | bytes accessed | tf_op | source)
XLA Modules:
  0.0 92.9 jit_solution(5915509073144987792)
XLA Ops:
  0.0 90.9 %shard_map.118 = bf16[8,128,2048]{2,1,0:T(8,128)(2,1)S(1)} custom-call(s32[8]{0:T(128)} %lengths.1, f32[1,128]{1,0:T(1,128)} %constant.4.frequencies, f32[1,2048]{1,0:T(1,128)} %bitcast.8, f32[1,1024]{1,0:T(1,128)} %bitcast.10, f32[1,128]{1,0:T(1,128)} %bitcast.11, f32[1,2048]{1,0:T(1,128)} %bitcast.9, bf16[8,128,2048]{2,1,0:T(8,128)(2,1)} %bitcast.7, ...), custom_call_target="tpu_custom_call" | custom-call | flops 12000000000 | bytes 26214400 | tf_op jit(solution)/shard_map/pallas_call | solution.py:506
  90.9 2.0 %copy.14 = bf16[1024,2048]{1,0:T(8,128)(2,1)} copy(bf16[1024,2048]{1,0:T(8,128)(2,1)S(1)} %bitcast.6) | data formatting | bytes 8388608

commit v4 on v3

--- a/solution.py
+++ b/solution.py
@@ -16,7 +16,7 @@
 ROWS_HERE = 8
 OWN = 8
 QW = OWN * HD
-WIDE = QW + 2 * HD
+WIDE = QW + HD
 SPAN = 2048
 TILE = 512
 FEATS = 2048
@@ -40,28 +40,30 @@
 TOPS = FAR + CHUNK_ROWS
 ZAG = TOPS + CHUNK_ROWS
 CAG = ZAG + 3
-RS1 = CAG + 1
+SQC = CAG + 1
+SQZ = SQC + 1
+RS1 = SQZ + 1
 RS2 = RS1 + 4
 AG2 = RS2 + 2
 AG1 = AG2 + 2
 ARRIVALS = AG1 + 4
 CORE_OUT, ZRS_OUT, SWAP_OUT, FAR_OUT, ZAG_OUT, CAG_OUT = 0, 1, 2, 4, 5, 6
-RS1_OUT, RS2_OUT, AG2_OUT, AG1_OUT, TOPS_OUT = 7, 9, 11, 13, 15
-DEPARTURES = 16
+RS1_OUT, RS2_OUT, AG2_OUT, AG1_OUT, TOPS_OUT, SQC_OUT, SQZ_OUT = 7, 9, 11, 13, 15, 16, 17
+DEPARTURES = 18
 
 ORDER = (
-    (0, 0), (1, 0), (0, 1), (4, 0), (1, 1), (4, 1), (0, 2), (5, 0), (3, 0), (1, 2),
-    (6, 0), (3, 1), (2, 0), (6, 1), (2, 1), (1, 3), (3, 2), (0, 3), (7, 0), (5, 1),
-    (2, 2), (4, 2), (0, 4), (1, 4), (3, 3), (7, 1), (5, 2), (2, 3), (6, 2), (4, 3),
-    (0, 5), (7, 2), (3, 4), (5, 3), (1, 5), (2, 4), (6, 3), (0, 6), (4, 4), (7, 3),
-    (3, 5), (0, 7), (1, 6), (2, 5), (5, 4), (1, 7), (6, 4), (4, 5), (3, 6), (7, 4),
-    (0, 8), (2, 6), (1, 8), (2, 7), (3, 7), (7, 5), (5, 5), (6, 5), (0, 9), (4, 6),
-    (1, 9), (2, 8), (4, 7), (3, 8), (7, 6), (0, 10), (7, 7), (5, 6), (1, 10), (4, 8),
-    (6, 6), (5, 7), (6, 7), (7, 8), (3, 9), (4, 9), (1, 11), (5, 8), (7, 9), (2, 9),
-    (6, 8), (0, 11), (4, 10), (3, 10), (5, 9), (6, 9), (2, 10), (1, 12), (7, 10), (0, 12),
-    (5, 10), (4, 11), (6, 10), (3, 11), (5, 11), (2, 11), (7, 11), (6, 11), (1, 13), (4, 12),
-    (2, 12), (3, 12), (5, 12), (7, 12), (6, 12), (4, 13), (2, 13), (0, 13), (7, 13), (5, 13),
-    (3, 13), (6, 13),
+    (0, 0), (1, 0), (0, 1), (3, 0), (1, 1), (2, 0), (7, 0), (3, 1), (4, 0), (0, 2),
+    (1, 2), (5, 0), (2, 1), (3, 2), (4, 1), (0, 3), (1, 3), (2, 2), (5, 1), (6, 0),
+    (3, 3), (4, 2), (6, 1), (0, 4), (2, 3), (5, 2), (7, 1), (1, 4), (3, 4), (4, 3),
+    (6, 2), (0, 5), (5, 3), (2, 4), (7, 2), (1, 5), (3, 5), (6, 3), (4, 4), (0, 6),
+    (5, 4), (2, 5), (7, 3), (0, 7), (1, 6), (6, 4), (3, 6), (1, 7), (5, 5), (7, 4),
+    (2, 6), (4, 5), (0, 8), (3, 7), (2, 7), (6, 5), (5, 6), (1, 8), (7, 5), (0, 9),
+    (4, 6), (5, 7), (2, 8), (4, 7), (6, 6), (7, 6), (0, 10), (3, 8), (7, 7), (6, 7),
+    (1, 9), (5, 8), (3, 9), (2, 9), (4, 8), (0, 11), (5, 9), (6, 8), (3, 10), (1, 10),
+    (4, 9), (7, 8), (0, 12), (2, 10), (5, 10), (6, 9), (4, 10), (7, 9), (1, 11), (5, 11),
+    (4, 11), (7, 10), (6, 10), (0, 13), (2, 11), (3, 11), (5, 12), (6, 11), (7, 11), (2, 12),
+    (1, 12), (4, 12), (3, 12), (6, 12), (7, 12), (3, 13), (6, 13), (4, 13), (1, 13), (5, 13),
+    (2, 13), (7, 13),
 )
 
 
@@ -89,7 +91,7 @@
     out,
     cosines, sines,
     xs, wq_v, wkv_v, wo_v, k_v, v_v, scaled,
-    ybuf, crecv, zrecv, qbuf, kvbuf, kpad, vpad, obuf, osend, orecv, tops, trecv, gat,
+    ybuf, crecv, zrecv, squares, landed, inverses, qbuf, kvbuf, kpad, vpad, obuf, osend, orecv, tops, trecv, gat,
     pbuf,
     load_sem, send_sem, recv_sem,
     *sides,
@@ -211,7 +213,9 @@
     def project(c):
         states_load(c).wait()
         wide = f32(xs[c]).reshape(M, FEATS)
-        squares = jnp.sum(wide * wide, axis=1, keepdims=True)
+        column = jnp.sum(wide * wide, axis=1, keepdims=True)
+        squares[c, 0] = jnp.broadcast_to(column, (M, M)).T[0:1]
+        send(squares.at[c, 0], landed.at[c, 0], SQC_OUT, SQC, c, core_peer)
         scaled[...] = (wide * gain[...]).astype(jnp.bfloat16)
         if c == 0:
             wq_load.wait()
@@ -221,7 +225,6 @@
             for b in range(NB):
                 ybuf[c, b % 2, b // 2, :, start] = block[b * T : (b + 1) * T]
 
-        put(jnp.broadcast_to(squares, (M, HD)), pl.ds(QW + HD, HD))
         put(
             jnp.dot(scaled[...], wkv_v[...], preferred_element_type=jnp.float32), pl.ds(QW, HD)
         )
@@ -236,13 +239,23 @@
         arrived(crecv.at[c], CORE, c)
         ybuf[c, core] = ybuf[c, core] + crecv[c]
         scatter_start(ZRS_OUT, ZRS, c, z_shard(c), zrecv.at[c], z, z_plus, z_minus)
+        arrived(landed.at[c, 0], SQC, c)
+        squares[c, 1] = squares[c, 0] + landed[c, 0]
+        own = squares.at[c, 1]
+        to_ring(
+            SQZ_OUT, (SQZ,) * 3, c, lambda step: own, lambda k: landed.at[c, k + 1], z, z_ring
+        )
 
     def project_mid(c):
         scatter_mid(ZRS_OUT, ZRS, c, z_shard(c), zrecv.at[c], z, z_plus, z_minus)
 
     def project_end(c):
         total = jnp.concatenate(scatter_end(ZRS, c, z_shard(c), zrecv.at[c], z), axis=0)
-        inverse = lax.rsqrt(total[:, QW + HD :] / D + 1e-05)
+        arrived(landed.at[c, pl.ds(1, 3)], SQZ, c)
+        summed = squares[c, 1] + landed[c, 1] + landed[c, 2] + landed[c, 3]
+        row = lax.rsqrt(summed / D + 1e-05)
+        inverses[...] = jnp.broadcast_to(row, (M, M)).T
+        inverse = inverses[pl.ds(pl.multiple_of(din * T, T), T)]
         cosine = cosines[c * T : (c + 1) * T]
         sine = sines[c * T : (c + 1) * T]
         half = HD // 2
@@ -470,6 +483,8 @@
 
     for c in range(NC):
         departed(crecv.at[c], CORE_OUT, c)
+        departed(landed.at[c, 0], SQC_OUT, c)
+        departed(landed.at[c, pl.ds(1, 3)], SQZ_OUT, c)
         departed(zrecv.at[c], ZRS_OUT, c)
         departed(qbuf.at[c, 0], SWAP_OUT, c)
         departed(kvbuf.at[c, 0], SWAP_OUT + 1, c)
@@ -521,6 +536,9 @@
             pltpu.VMEM((NC, 2, 4, T, WIDE), jnp.float32),
             pltpu.VMEM((NC, 4, T, WIDE), jnp.float32),
             pltpu.VMEM((NC, 6, T // 2, WIDE), jnp.float32),
+            pltpu.VMEM((NC, 2, 1, M), jnp.float32),
+            pltpu.VMEM((NC, 4, 1, M), jnp.float32),
+            pltpu.VMEM((M, M), jnp.float32),
             pltpu.VMEM((NC, 2, CHUNK_ROWS, OWN * DRAFT, HD), bf16),
             pltpu.VMEM((NC, 2, T, HD), bf16),
             pltpu.VMEM((CHUNK_ROWS, HD, HD), bf16),

time: 93.3 us -> 91 us (0.975)
  Pallas kernels: 90.9 us -> 88.8 us
    pallas_call x1, Pallas kernels: 90.9 us -> 88.8 us  [shards(): pl.pallas_call(kernel, out_shape=pltpu.VMEM((NB, ROWS_HERE * DRAFT, OUTS)...]
where the time goes in v4:
time: 91 us; the launch traced here: 90.8 us
  Pallas kernels  88.8 us (98%)
  local copies, waits for them, and re-layouts  2.02 us (2%)
    pallas_call x1, Pallas kernels, shards(): pl.pallas_call(kernel, out_shape=pltpu.VMEM((NB, ROWS_HERE * DRAFT, OUTS)...  88.8 us
    unnamed x1, local copies, waits for them, and re-layouts  2.02 us

profile of v4, /device:TPU:0, one launch (start us, length us, event | category | flops | bytes accessed | tf_op | source)
XLA Modules:
  0.0 90.8 jit_solution(16680992729739947759)
XLA Ops:
  0.0 88.8 %shard_map.118 = bf16[8,128,2048]{2,1,0:T(8,128)(2,1)S(1)} custom-call(s32[8]{0:T(128)} %lengths.1, f32[1,128]{1,0:T(1,128)} %constant.4.frequencies, f32[1,2048]{1,0:T(1,128)} %bitcast.8, f32[1,1024]{1,0:T(1,128)} %bitcast.10, f32[1,128]{1,0:T(1,128)} %bitcast.11, f32[1,2048]{1,0:T(1,128)} %bitcast.9, bf16[8,128,2048]{2,1,0:T(8,128)(2,1)} %bitcast.7, ...), custom_call_target="tpu_custom_call" | custom-call | flops 12000000000 | bytes 26214400 | tf_op jit(solution)/shard_map/pallas_call | solution.py:521
  88.8 2.0 %copy.14 = bf16[1024,2048]{1,0:T(8,128)(2,1)} copy(bf16[1024,2048]{1,0:T(8,128)(2,1)S(1)} %bitcast.6) | data formatting | bytes 8388608

commit v5 on v4

--- a/solution.py
+++ b/solution.py
@@ -396,7 +396,7 @@
         arrived(gat.at[c, pl.ds(0, 4)], CAG, c)
 
         heads = gat[c].reshape(M, QW)
-        for side in range(2):
+        for side in (1, 0):
             width = OUTS // 2
             cols = slice(side * width, (side + 1) * width)
             block = jnp.dot(heads, wo_v[:, cols], preferred_element_type=jnp.float32)

time: 91 us -> 91.7 us (level)
  no operation moved by 1% of the time
where the time goes in v5:
time: 91.7 us; the launch traced here: 90.8 us
  Pallas kernels  88.8 us (97%)
  local copies, waits for them, and re-layouts  2.02 us (2%)
    pallas_call x1, Pallas kernels, shards(): pl.pallas_call(kernel, out_shape=pltpu.VMEM((NB, ROWS_HERE * DRAFT, OUTS)...  88.8 us
    unnamed x1, local copies, waits for them, and re-layouts  2.02 us

profile of v5, /device:TPU:0, one launch (start us, length us, event | category | flops | bytes accessed | tf_op | source)
XLA Modules:
  0.0 90.8 jit_solution(6317894669806282690)
XLA Ops:
  0.0 88.8 %shard_map.118 = bf16[8,128,2048]{2,1,0:T(8,128)(2,1)S(1)} custom-call(s32[8]{0:T(128)} %lengths.1, f32[1,128]{1,0:T(1,128)} %constant.4.frequencies, f32[1,2048]{1,0:T(1,128)} %bitcast.8, f32[1,1024]{1,0:T(1,128)} %bitcast.10, f32[1,128]{1,0:T(1,128)} %bitcast.11, f32[1,2048]{1,0:T(1,128)} %bitcast.9, bf16[8,128,2048]{2,1,0:T(8,128)(2,1)} %bitcast.7, ...), custom_call_target="tpu_custom_call" | custom-call | flops 12000000000 | bytes 26214400 | tf_op jit(solution)/shard_map/pallas_call | solution.py:521
  88.8 2.0 %copy.14 = bf16[1024,2048]{1,0:T(8,128)(2,1)} copy(bf16[1024,2048]{1,0:T(8,128)(2,1)S(1)} %bitcast.6) | data formatting | bytes 8388608
